TPU v7x, 512 devices: a whole 4x4x16 slice. The times are simulated.
512 devices in a mesh: tm: 32 (over y, z_lo, core), space: 16 (over x, z_hi).
Axes of the slice: x: 4, y: 4, z: 16 (z_hi: 4, z_lo: 4; z = z_hi * 4 + z_lo), core: 2. Of those that a mesh axis runs over, the one named last changes fastest.
Arguments:
- old_nodes: float32 [32, 5, 4, 96, 8, 128], P('tm', None, None, 'space'), may hold values from -6 to 6
- initial: float32 [4, 96, 8, 128], P(None, 'space'), may hold values from -6 to 6
- shear_modulus: float32 [96, 8, 128], P('space'), may hold values from 0.2 to 1
- mobility: float32 [96, 8, 128], P('space'), may hold values from 0.2 to 1
Outputs:
- new_nodes: float32 [32, 5, 4, 96, 8, 128], P('tm', None, None, 'space')
- next_start: float32 [32, 4, 96, 8, 128], P('tm', None, 'space')
All inputs are finite; a program needn't handle non-finite values.
Results may differ from a plain program's by a relative error of at most 0.00002.
Values sent between devices are 32-bit elements; how exact they have to be, the bound alone decides.
A program may use at most 64 MiB of HBM per device.

v0:
```python
import math

import jax
import jax.numpy as jnp
from jax import lax
from jax.sharding import PartitionSpec as P

coupling = 0.5
slice_step = 0.4


def from_behind(value, axis, steps):
    count = lax.axis_size(axis)
    first, last = (max(0, -steps), min(count, count - steps))
    return lax.ppermute(value, axis, [(source, source + steps) for source in range(first, last)])


def padded_2(array, sides, width):
    for axis, dim in sides:
        peers, length = (lax.axis_size(axis), array.shape[dim])
        up = [(i, (i + 1) % peers) for i in range(peers - 1)]
        down = [(j, i) for i, j in up]
        last = lax.slice_in_dim(array, length - width, length, axis=dim)
        first = lax.slice_in_dim(array, 0, width, axis=dim)
        before = lax.ppermute(last, axis, up)
        after = lax.ppermute(first, axis, down)
        array = jnp.concatenate([before, array, after], axis=dim)
    return array


def node_tables():
    root_gap = math.sqrt(3.0 / 7.0)
    points = [0.0, (1.0 - root_gap) / 2.0, 0.5, (1.0 + root_gap) / 2.0, 1.0]
    polys = []
    for node in range(5):
        coeffs = [1.0]
        for other in range(5):
            if other != node:
                denom = points[node] - points[other]
                grown = [0.0] * (len(coeffs) + 1)
                for power in range(len(coeffs)):
                    grown[power + 1] += coeffs[power] / denom
                    grown[power] -= points[other] * coeffs[power] / denom
                coeffs = grown
        polys.append(coeffs)
    integral = []
    for column in range(4):
        lower = points[column]
        upper = points[column + 1]
        table_row = []
        for node in range(5):
            total = 0.0
            for power in range(5):
                total += (
                    polys[node][power] * (upper ** (power + 1) - lower ** (power + 1)) / (power + 1)
                )
            table_row.append(total * slice_step)
        integral.append(table_row)
    widths = [(points[column + 1] - points[column]) * slice_step for column in range(4)]
    return (integral, widths)


def component(source, number):
    return source[..., number, :, :, :]


def operator(padz, stiffness, fluidity, lap_scale, grad_scale):
    padded = jnp.pad(padz, [(0, 0)] * (padz.ndim - 2) + [(1, 1), (1, 1)])
    center = padded[..., 1:-1, 1:-1, 1:-1]
    z_plus = padded[..., 2:, 1:-1, 1:-1]
    z_minus = padded[..., :-2, 1:-1, 1:-1]
    x_plus = padded[..., 1:-1, 2:, 1:-1]
    x_minus = padded[..., 1:-1, :-2, 1:-1]
    y_plus = padded[..., 1:-1, 1:-1, 2:]
    y_minus = padded[..., 1:-1, 1:-1, :-2]
    laplace = (z_plus + z_minus + x_plus + x_minus + y_plus + y_minus - 6.0 * center) * lap_scale
    grad_z = (component(z_plus, 3) - component(z_minus, 3)) * grad_scale
    grad_x = (component(x_plus, 3) - component(x_minus, 3)) * grad_scale
    grad_y = (component(y_plus, 3) - component(y_minus, 3)) * grad_scale
    diverge = (
        component(z_plus, 0)
        - component(z_minus, 0)
        + component(x_plus, 1)
        - component(x_minus, 1)
        + component(y_plus, 2)
        - component(y_minus, 2)
    ) * grad_scale
    return jnp.stack(
        [
            stiffness * component(laplace, 0) - coupling * grad_z,
            stiffness * component(laplace, 1) - coupling * grad_x,
            stiffness * component(laplace, 2) - coupling * grad_y,
            fluidity * component(laplace, 3) - coupling * diverge,
        ],
        axis=-4,
    )


def restrict(source):
    new_shape = source.shape[:-3] + (
        source.shape[-3] // 2,
        2,
        source.shape[-2] // 2,
        2,
        source.shape[-1] // 2,
        2,
    )
    return jnp.mean(source.reshape(new_shape), axis=(-5, -3, -1))


def prolong(source):
    return jnp.repeat(jnp.repeat(jnp.repeat(source, 2, -3), 2, -2), 2, -1)


def spread_sum(table_row, images):
    total = table_row[0] * images[0:1]
    for position in range(1, 5):
        total = total + table_row[position] * images[position : position + 1]
    return total


def fine_sweep(stacked, evaluate, inside, integral, widths):
    first_images = evaluate(stacked)
    old_f = first_images[1:]
    current = stacked[0:1]
    f_current = first_images[0:1]
    values = [current]
    images = []
    for column in range(4):
        advanced = (
            current
            + widths[column] * (f_current - old_f[column : column + 1])
            + spread_sum(integral[column], old_f)
        ) * inside
        images.append(f_current)
        values.append(advanced)
        current = advanced
        f_current = evaluate(advanced)
    images.append(f_current)
    return (jnp.concatenate(values, axis=0), jnp.concatenate(images, axis=0))


def on_device(old_nodes, initial, shear_modulus, mobility):
    integral, widths = node_tables()
    nodes_here = old_nodes[0]
    received = from_behind(nodes_here[4:5], "tm", 1)
    is_first = lax.axis_index("tm") == 0
    start_value = jnp.where(is_first, initial[None], received)
    stacked = jnp.concatenate([start_value, nodes_here], axis=0)

    def evaluate_near(source):
        padz = padded_2(source, (("space", 2),), 1)
        return operator(padz, shear_modulus, mobility, 1.0, 0.5)

    values, fine_f = fine_sweep(stacked, evaluate_near, 1.0, integral, widths)
    coarse_nodes = restrict(values)
    coarse_shear = restrict(shear_modulus)
    coarse_mobility = restrict(mobility)

    def coarse_eval(source):
        padz = padded_2(source, (("space", 2),), 1)
        return operator(padz, coarse_shear, coarse_mobility, 0.25, 0.25)

    coarse_old = coarse_eval(coarse_nodes[1:4])
    restricted = [restrict(spread_sum(integral[column], fine_f)) for column in range(4)]
    coarse_values = [coarse_nodes[0:1]]
    coarse_values.append(coarse_values[0] + restricted[0])
    for column in range(1, 4):
        now_value = coarse_values[column]
        coarse_values.append(
            now_value
            + widths[column] * (coarse_eval(now_value) - coarse_old[column - 1 : column])
            + restricted[column]
        )
    result = [start_value]
    for column in range(1, 5):
        result.append(
            values[column : column + 1]
            + prolong(coarse_values[column] - coarse_nodes[column : column + 1])
        )
    new_here = jnp.concatenate(result, axis=0)
    end_value = from_behind(new_here[4:5], "tm", 1)
    next_start = jnp.where(is_first, initial[None], end_value)
    return (new_here[None], next_start)


def solution(mesh):
    placed = (
        P("tm", None, None, "space", None, None),
        P(None, "space", None, None),
        P("space", None, None),
        P("space", None, None),
    )
    return jax.shard_map(
        on_device,
        mesh=mesh,
        in_specs=placed,
        out_specs=(P("tm", None, None, "space", None, None), P("tm", None, "space", None, None)),
        check_vma=False,
    )
```

profile of v0, /device:TPU:20, one launch (start us, length us, event | category | flops | bytes accessed | tf_op | source)
XLA Modules:
  0.0 228.2 jit_solution(10528773805356891067)
XLA Ops:
  0.6 1.0 slice_bitcast_fusion
  1.6 1.9 collective-permute-start
  3.5 6.7 %collective-permute-done = f32[1,4,6,8,128]{4,3,2,1,0:T(8,128)S(1)} collective-permute-done((f32[1,4,6,8,128]{4,3,2,1,0:T(8,128)S(1)}, f32[1,4,6,8,128]{4,3,2,1,0:T(8,128)S(1)}, u32[]{:S(2)}, u32[]{:S(2)}) %collective-permute-start) | collective-permute-done | bytes 98336 | tf_op jit(solution)/shard_map/ppermute | solution.py:15
  12.1 9.1 %collective-permute-start.2 = (f32[6,4,1,8,128]{4,3,2,1,0:T(8,128)S(1)}, f32[6,4,1,8,128]{4,3,2,1,0:T(8,128)S(1)}, u32[]{:S(2)}, u32[]{:S(2)}) collective-permute-start(f32[6,4,1,8,128]{4,3,2,1,0:T(8,128)S(1)} %get-tuple-element.55), channel_id=1, source_target_pairs={{0,1},{1,2},{2,3},{3,4},{4,5},{5,6},{6,7},{7,8},{8,9},{9,10},{10,1... | collective-permute-start | bytes 294920 | tf_op jit(solution)/shard_map/ppermute | solution.py:25
  21.2 5.5 %collective-permute-start.1 = (f32[6,4,1,8,128]{4,3,2,1,0:T(8,128)S(1)}, f32[6,4,1,8,128]{4,3,2,1,0:T(8,128)S(1)}, u32[]{:S(2)}, u32[]{:S(2)}) collective-permute-start(f32[6,4,1,8,128]{4,3,2,1,0:T(8,128)S(1)} %get-tuple-element.56), channel_id=1, source_target_pairs={{1,0},{2,1},{3,2},{4,3},{5,4},{6,5},{7,6},{8,7},{9,8},{10,9},{11,1... | collective-permute-start | bytes 294920 | tf_op jit(solution)/shard_map/ppermute | solution.py:26
  28.1 6.4 %collective-permute-done.1 = f32[6,4,1,8,128]{4,3,2,1,0:T(8,128)S(1)} collective-permute-done((f32[6,4,1,8,128]{4,3,2,1,0:T(8,128)S(1)}, f32[6,4,1,8,128]{4,3,2,1,0:T(8,128)S(1)}, u32[]{:S(2)}, u32[]{:S(2)}) %collective-permute-start.1) | collective-permute-done | bytes 98336 | tf_op jit(solution)/shard_map/ppermute | solution.py:26
  34.5 1.3 pad_maximum_fusion.1
  35.8 1.5 select_maximum_fusion
  38.5 7.8 %collective-permute-start.4 = (f32[1,4,1,8,128]{4,3,2,1,0:T(8,128)S(1)}, f32[1,4,1,8,128]{4,3,2,1,0:T(8,128)S(1)}, u32[]{:S(2)}, u32[]{:S(2)}) collective-permute-start(f32[1,4,1,8,128]{4,3,2,1,0:T(8,128)S(1)} %get-tuple-element.77), channel_id=1, source_target_pairs={{0,1},{1,2},{2,3},{3,4},{4,5},{5,6},{6,7},{7,8},{8,9},{9,10},{10,1... | collective-permute-start | bytes 49160 | tf_op jit(solution)/shard_map/ppermute | solution.py:25
  46.3 2.9 %collective-permute-start.3 = (f32[1,4,1,8,128]{4,3,2,1,0:T(8,128)S(1)}, f32[1,4,1,8,128]{4,3,2,1,0:T(8,128)S(1)}, u32[]{:S(2)}, u32[]{:S(2)}) collective-permute-start(f32[1,4,1,8,128]{4,3,2,1,0:T(8,128)S(1)} %get-tuple-element.78), channel_id=1, source_target_pairs={{1,0},{2,1},{3,2},{4,3},{5,4},{6,5},{7,6},{8,7},{9,8},{10,9},{11,1... | collective-permute-start | bytes 49160 | tf_op jit(solution)/shard_map/ppermute | solution.py:26
  49.1 6.7 %collective-permute-done.3 = f32[1,4,1,8,128]{4,3,2,1,0:T(8,128)S(1)} collective-permute-done((f32[1,4,1,8,128]{4,3,2,1,0:T(8,128)S(1)}, f32[1,4,1,8,128]{4,3,2,1,0:T(8,128)S(1)}, u32[]{:S(2)}, u32[]{:S(2)}) %collective-permute-start.3) | collective-permute-done | bytes 16416 | tf_op jit(solution)/shard_map/ppermute | solution.py:26
  56.4 5.5 %collective-permute-start.6 = (f32[1,4,1,8,128]{4,3,2,1,0:T(8,128)S(1)}, f32[1,4,1,8,128]{4,3,2,1,0:T(8,128)S(1)}, u32[]{:S(2)}, u32[]{:S(2)}) collective-permute-start(f32[1,4,1,8,128]{4,3,2,1,0:T(8,128)S(1)} %get-tuple-element.75), channel_id=1, source_target_pairs={{0,1},{1,2},{2,3},{3,4},{4,5},{5,6},{6,7},{7,8},{8,9},{9,10},{10,1... | collective-permute-start | bytes 49160 | tf_op jit(solution)/shard_map/ppermute | solution.py:25
  61.9 5.1 %collective-permute-start.5 = (f32[1,4,1,8,128]{4,3,2,1,0:T(8,128)S(1)}, f32[1,4,1,8,128]{4,3,2,1,0:T(8,128)S(1)}, u32[]{:S(2)}, u32[]{:S(2)}) collective-permute-start(f32[1,4,1,8,128]{4,3,2,1,0:T(8,128)S(1)} %get-tuple-element.76), channel_id=1, source_target_pairs={{1,0},{2,1},{3,2},{4,3},{5,4},{6,5},{7,6},{8,7},{9,8},{10,9},{11,1... | collective-permute-start | bytes 49160 | tf_op jit(solution)/shard_map/ppermute | solution.py:26
  67.1 2.7 %reshape.1493 = f32[3,2,4,2,64,2]{5,4,3,2,1,0:T(8,128)} reshape(f32[6,8,128]{2,1,0:T(8,128)S(1)} %copy-done.8) | data formatting | bytes 49152 | tf_op jit(solution)/shard_map/reshape | solution.py:108
  69.8 1.5 reshape.1492
  71.4 1.6 reduce_sum.66
  73.8 4.6 %collective-permute-start.8 = (f32[1,4,1,8,128]{4,3,2,1,0:T(8,128)S(1)}, f32[1,4,1,8,128]{4,3,2,1,0:T(8,128)S(1)}, u32[]{:S(2)}, u32[]{:S(2)}) collective-permute-start(f32[1,4,1,8,128]{4,3,2,1,0:T(8,128)S(1)} %get-tuple-element.73), channel_id=1, source_target_pairs={{0,1},{1,2},{2,3},{3,4},{4,5},{5,6},{6,7},{7,8},{8,9},{9,10},{10,1... | collective-permute-start | bytes 49160 | tf_op jit(solution)/shard_map/ppermute | solution.py:25
  78.4 6.0 %collective-permute-start.7 = (f32[1,4,1,8,128]{4,3,2,1,0:T(8,128)S(1)}, f32[1,4,1,8,128]{4,3,2,1,0:T(8,128)S(1)}, u32[]{:S(2)}, u32[]{:S(2)}) collective-permute-start(f32[1,4,1,8,128]{4,3,2,1,0:T(8,128)S(1)} %get-tuple-element.74), channel_id=1, source_target_pairs={{1,0},{2,1},{3,2},{4,3},{5,4},{6,5},{7,6},{8,7},{9,8},{10,9},{11,1... | collective-permute-start | bytes 49160 | tf_op jit(solution)/shard_map/ppermute | solution.py:26
  84.4 3.5 %collective-permute-done.7 = f32[1,4,1,8,128]{4,3,2,1,0:T(8,128)S(1)} collective-permute-done((f32[1,4,1,8,128]{4,3,2,1,0:T(8,128)S(1)}, f32[1,4,1,8,128]{4,3,2,1,0:T(8,128)S(1)}, u32[]{:S(2)}, u32[]{:S(2)}) %collective-permute-start.7) | collective-permute-done | bytes 16416 | tf_op jit(solution)/shard_map/ppermute | solution.py:26
  88.5 6.8 %copy.1209 = f32[5,4,6,8,128]{0,4,3,2,1:T(8,128)} copy(f32[5,4,6,8,128]{4,3,2,1,0:T(8,128)S(1)} %get-tuple-element.28) | data formatting | bytes 983040 | tf_op jit(solution)/shard_map/concatenate | solution.py:140
  95.3 12.3 %reduce_sum.63 = f32[5,4,3,4,64]{0,4,3,2,1:T(8,128)S(1)} reduce(f32[5,4,3,2,4,2,64,2]{0,7,6,5,4,3,2,1:T(2,128)} %bitcast.282, f32[]{:T(128)} %constant.82.clone.1), dimensions={3,5,7}, to_apply=%region_0.1 | reduce | flops 107520 | bytes 552964 | tf_op jit(solution)/shard_map/reduce_sum | solution.py:108
  108.1 2.4 %collective-permute-start.14 = (f32[3,4,1,4,64]{4,3,2,1,0:T(4,128)S(1)}, f32[3,4,1,4,64]{4,3,2,1,0:T(4,128)S(1)}, u32[]{:S(2)}, u32[]{:S(2)}) collective-permute-start(f32[3,4,1,4,64]{4,3,2,1,0:T(4,128)S(1)} %get-tuple-element.60), channel_id=1, source_target_pairs={{0,1},{1,2},{2,3},{3,4},{4,5},{5,6},{6,7},{7,8},{8,9},{9,10},{10,1... | collective-permute-start | bytes 36872 | tf_op jit(solution)/shard_map/ppermute | solution.py:25
  110.5 8.3 %collective-permute-start.13 = (f32[3,4,1,4,64]{4,3,2,1,0:T(4,128)S(1)}, f32[3,4,1,4,64]{4,3,2,1,0:T(4,128)S(1)}, u32[]{:S(2)}, u32[]{:S(2)}) collective-permute-start(f32[3,4,1,4,64]{4,3,2,1,0:T(4,128)S(1)} %get-tuple-element.61), channel_id=1, source_target_pairs={{1,0},{2,1},{3,2},{4,3},{5,4},{6,5},{7,6},{8,7},{9,8},{10,9},{11,1... | collective-permute-start | bytes 36872 | tf_op jit(solution)/shard_map/ppermute | solution.py:26
  118.8 1.9 collective-permute-start.10
  120.8 8.9 %collective-permute-start.9 = (f32[1,4,1,8,128]{4,3,2,1,0:T(8,128)S(1)}, f32[1,4,1,8,128]{4,3,2,1,0:T(8,128)S(1)}, u32[]{:S(2)}, u32[]{:S(2)}) collective-permute-start(f32[1,4,1,8,128]{4,3,2,1,0:T(8,128)S(1)} %get-tuple-element.72), channel_id=1, source_target_pairs={{1,0},{2,1},{3,2},{4,3},{5,4},{6,5},{7,6},{8,7},{9,8},{10,9},{11,1... | collective-permute-start | bytes 49160 | tf_op jit(solution)/shard_map/ppermute | solution.py:26
  134.2 1.8 copy.1211
  136.0 3.6 %reduce_sum.64 = f32[4,3,4,64]{0,3,2,1:T(8,128)} reduce(f32[4,3,2,4,2,64,2]{0,6,5,4,3,2,1:T(2,128)S(1)} %bitcast.290, f32[]{:T(128)} %constant.82.clone.1), dimensions={2,4,6}, to_apply=%region_1.2 | reduce | flops 21504 | bytes 110596 | tf_op jit(solution)/shard_map/reduce_sum | solution.py:108
  139.6 1.0 broadcast_multiply_fusion.3
  141.4 1.8 copy.1223
  143.3 3.6 %reduce_sum.69 = f32[4,3,4,64]{0,3,2,1:T(8,128)} reduce(f32[4,3,2,4,2,64,2]{0,6,5,4,3,2,1:T(2,128)S(1)} %bitcast.291, f32[]{:T(128)} %constant.82.clone.1), dimensions={2,4,6}, to_apply=%region_6.7 | reduce | flops 21504 | bytes 110596 | tf_op jit(solution)/shard_map/reduce_sum | solution.py:108
  146.9 1.8 broadcast_multiply_fusion
  148.7 1.8 copy.1219
  150.5 3.6 %reduce_sum.68 = f32[4,3,4,64]{0,3,2,1:T(8,128)} reduce(f32[4,3,2,4,2,64,2]{0,6,5,4,3,2,1:T(2,128)S(1)} %bitcast.292, f32[]{:T(128)} %constant.82.clone.1), dimensions={2,4,6}, to_apply=%region_5.6 | reduce | flops 21504 | bytes 110596 | tf_op jit(solution)/shard_map/reduce_sum | solution.py:108
  154.1 1.8 broadcast_multiply_fusion.1
  155.9 2.1 copy.1215
  158.0 3.6 %reduce_sum.67 = f32[4,3,4,64]{0,3,2,1:T(8,128)} reduce(f32[4,3,2,4,2,64,2]{0,6,5,4,3,2,1:T(2,128)S(1)} %bitcast.289, f32[]{:T(128)} %constant.82.clone.1), dimensions={2,4,6}, to_apply=%region_4.5 | reduce | flops 21504 | bytes 110596 | tf_op jit(solution)/shard_map/reduce_sum | solution.py:108
  161.6 1.8 broadcast_multiply_fusion.2
  164.9 5.4 %collective-permute-start.12 = (f32[1,4,1,4,64]{4,3,2,1,0:T(4,128)}, f32[1,4,1,4,64]{4,3,2,1,0:T(4,128)}, u32[]{:S(2)}, u32[]{:S(2)}) collective-permute-start(f32[1,4,1,4,64]{4,3,2,1,0:T(4,128)} %get-tuple-element.83), channel_id=1, source_target_pairs={{0,1},{1,2},{2,3},{3,4},{4,5},{5,6},{6,7},{7,8},{8,9},{9,10},{10,1... | collective-permute-start | bytes 12296 | tf_op jit(solution)/shard_map/ppermute | solution.py:25
  170.3 5.6 %collective-permute-start.11 = (f32[1,4,1,4,64]{4,3,2,1,0:T(4,128)}, f32[1,4,1,4,64]{4,3,2,1,0:T(4,128)}, u32[]{:S(2)}, u32[]{:S(2)}) collective-permute-start(f32[1,4,1,4,64]{4,3,2,1,0:T(4,128)} %get-tuple-element.84), channel_id=1, source_target_pairs={{1,0},{2,1},{3,2},{4,3},{5,4},{6,5},{7,6},{8,7},{9,8},{10,9},{11,1... | collective-permute-start | bytes 12296 | tf_op jit(solution)/shard_map/ppermute | solution.py:26
  178.3 1.2 copy.1228
  183.2 7.2 %collective-permute-start.16 = (f32[1,4,1,4,64]{4,3,2,1,0:T(4,128)S(1)}, f32[1,4,1,4,64]{4,3,2,1,0:T(4,128)S(1)}, u32[]{:S(2)}, u32[]{:S(2)}) collective-permute-start(f32[1,4,1,4,64]{4,3,2,1,0:T(4,128)S(1)} %get-tuple-element.81), channel_id=1, source_target_pairs={{0,1},{1,2},{2,3},{3,4},{4,5},{5,6},{6,7},{7,8},{8,9},{9,10},{10,1... | collective-permute-start | bytes 12296 | tf_op jit(solution)/shard_map/ppermute | solution.py:25
  190.4 3.4 %collective-permute-start.15 = (f32[1,4,1,4,64]{4,3,2,1,0:T(4,128)S(1)}, f32[1,4,1,4,64]{4,3,2,1,0:T(4,128)S(1)}, u32[]{:S(2)}, u32[]{:S(2)}) collective-permute-start(f32[1,4,1,4,64]{4,3,2,1,0:T(4,128)S(1)} %get-tuple-element.82), channel_id=1, source_target_pairs={{1,0},{2,1},{3,2},{4,3},{5,4},{6,5},{7,6},{8,7},{9,8},{10,9},{11,1... | collective-permute-start | bytes 12296 | tf_op jit(solution)/shard_map/ppermute | solution.py:26
  195.9 4.0 %collective-permute-done.15 = f32[1,4,1,4,64]{4,3,2,1,0:T(4,128)S(1)} collective-permute-done((f32[1,4,1,4,64]{4,3,2,1,0:T(4,128)S(1)}, f32[1,4,1,4,64]{4,3,2,1,0:T(4,128)S(1)}, u32[]{:S(2)}, u32[]{:S(2)}) %collective-permute-start.15) | collective-permute-done | bytes 4128 | tf_op jit(solution)/shard_map/ppermute | solution.py:26
  200.3 6.9 %collective-permute-start.18 = (f32[1,4,1,4,64]{4,3,2,1,0:T(4,128)S(1)}, f32[1,4,1,4,64]{4,3,2,1,0:T(4,128)S(1)}, u32[]{:S(2)}, u32[]{:S(2)}) collective-permute-start(f32[1,4,1,4,64]{4,3,2,1,0:T(4,128)S(1)} %get-tuple-element.79), channel_id=1, source_target_pairs={{0,1},{1,2},{2,3},{3,4},{4,5},{5,6},{6,7},{7,8},{8,9},{9,10},{10,1... | collective-permute-start | bytes 12296 | tf_op jit(solution)/shard_map/ppermute | solution.py:25
  207.1 3.8 %collective-permute-start.17 = (f32[1,4,1,4,64]{4,3,2,1,0:T(4,128)S(1)}, f32[1,4,1,4,64]{4,3,2,1,0:T(4,128)S(1)}, u32[]{:S(2)}, u32[]{:S(2)}) collective-permute-start(f32[1,4,1,4,64]{4,3,2,1,0:T(4,128)S(1)} %get-tuple-element.80), channel_id=1, source_target_pairs={{1,0},{2,1},{3,2},{4,3},{5,4},{6,5},{7,6},{8,7},{9,8},{10,9},{11,1... | collective-permute-start | bytes 12296 | tf_op jit(solution)/shard_map/ppermute | solution.py:26
  212.9 3.6 %collective-permute-done.17 = f32[1,4,1,4,64]{4,3,2,1,0:T(4,128)S(1)} collective-permute-done((f32[1,4,1,4,64]{4,3,2,1,0:T(4,128)S(1)}, f32[1,4,1,4,64]{4,3,2,1,0:T(4,128)S(1)}, u32[]{:S(2)}, u32[]{:S(2)}) %collective-permute-start.17) | collective-permute-done | bytes 4128 | tf_op jit(solution)/shard_map/ppermute | solution.py:26
  218.9 1.9 collective-permute-start.19
  220.9 6.7 %collective-permute-done.19 = f32[1,4,6,8,128]{4,3,2,1,0:T(8,128)S(1)} collective-permute-done((f32[1,4,6,8,128]{4,3,2,1,0:T(8,128)S(1)}, f32[1,4,6,8,128]{4,3,2,1,0:T(8,128)S(1)}, u32[]{:S(2)}, u32[]{:S(2)}) %collective-permute-start.19) | collective-permute-done | bytes 98336 | tf_op jit(solution)/shard_map/ppermute | solution.py:15
  (128 shorter events, 26.7 us)
Async XLA Ops:
  0.6 35.1 %copy-start = (f32[1,5,4,6,8,128]{5,4,3,2,1,0:T(8,128)S(1)}, f32[1,5,4,6,8,128]{5,4,3,2,1,0:T(8,128)}, u32[]{:S(2)}) copy-start(f32[1,5,4,6,8,128]{5,4,3,2,1,0:T(8,128)} %param.4) | copy-start | bytes 1474564
  1.6 8.6 %collective-permute-start = (f32[1,4,6,8,128]{4,3,2,1,0:T(8,128)S(1)}, f32[1,4,6,8,128]{4,3,2,1,0:T(8,128)S(1)}, u32[]{:S(2)}, u32[]{:S(2)}) collective-permute-start(f32[1,4,6,8,128]{4,3,2,1,0:T(8,128)S(1)} %slice_bitcast_fusion), channel_id=1, source_target_pairs={{0,16},{16,32},{32,48},{48,64},{64,80},{80,96},{96,112},{112,128},... | collective-permute-start | bytes 294920 | tf_op jit(solution)/shard_map/ppermute | solution.py:15
  12.1 16.0 %collective-permute-start.2 = (f32[6,4,1,8,128]{4,3,2,1,0:T(8,128)S(1)}, f32[6,4,1,8,128]{4,3,2,1,0:T(8,128)S(1)}, u32[]{:S(2)}, u32[]{:S(2)}) collective-permute-start(f32[6,4,1,8,128]{4,3,2,1,0:T(8,128)S(1)} %get-tuple-element.55), channel_id=1, source_target_pairs={{0,1},{1,2},{2,3},{3,4},{4,5},{5,6},{6,7},{7,8},{8,9},{9,10},{10,1... | collective-permute-start | bytes 294920 | tf_op jit(solution)/shard_map/ppermute | solution.py:25
  21.2 13.3 %collective-permute-start.1 = (f32[6,4,1,8,128]{4,3,2,1,0:T(8,128)S(1)}, f32[6,4,1,8,128]{4,3,2,1,0:T(8,128)S(1)}, u32[]{:S(2)}, u32[]{:S(2)}) collective-permute-start(f32[6,4,1,8,128]{4,3,2,1,0:T(8,128)S(1)} %get-tuple-element.56), channel_id=1, source_target_pairs={{1,0},{2,1},{3,2},{4,3},{5,4},{6,5},{7,6},{8,7},{9,8},{10,9},{11,1... | collective-permute-start | bytes 294920 | tf_op jit(solution)/shard_map/ppermute | solution.py:26
  37.2 0.7 copy-start.1
  37.3 0.8 copy-start.8
  38.5 10.7 %collective-permute-start.4 = (f32[1,4,1,8,128]{4,3,2,1,0:T(8,128)S(1)}, f32[1,4,1,8,128]{4,3,2,1,0:T(8,128)S(1)}, u32[]{:S(2)}, u32[]{:S(2)}) collective-permute-start(f32[1,4,1,8,128]{4,3,2,1,0:T(8,128)S(1)} %get-tuple-element.77), channel_id=1, source_target_pairs={{0,1},{1,2},{2,3},{3,4},{4,5},{5,6},{6,7},{7,8},{8,9},{9,10},{10,1... | collective-permute-start | bytes 49160 | tf_op jit(solution)/shard_map/ppermute | solution.py:25
  46.3 9.6 %collective-permute-start.3 = (f32[1,4,1,8,128]{4,3,2,1,0:T(8,128)S(1)}, f32[1,4,1,8,128]{4,3,2,1,0:T(8,128)S(1)}, u32[]{:S(2)}, u32[]{:S(2)}) collective-permute-start(f32[1,4,1,8,128]{4,3,2,1,0:T(8,128)S(1)} %get-tuple-element.78), channel_id=1, source_target_pairs={{1,0},{2,1},{3,2},{4,3},{5,4},{6,5},{7,6},{8,7},{9,8},{10,9},{11,1... | collective-permute-start | bytes 49160 | tf_op jit(solution)/shard_map/ppermute | solution.py:26
  56.4 16.8 %collective-permute-start.6 = (f32[1,4,1,8,128]{4,3,2,1,0:T(8,128)S(1)}, f32[1,4,1,8,128]{4,3,2,1,0:T(8,128)S(1)}, u32[]{:S(2)}, u32[]{:S(2)}) collective-permute-start(f32[1,4,1,8,128]{4,3,2,1,0:T(8,128)S(1)} %get-tuple-element.75), channel_id=1, source_target_pairs={{0,1},{1,2},{2,3},{3,4},{4,5},{5,6},{6,7},{7,8},{8,9},{9,10},{10,1... | collective-permute-start | bytes 49160 | tf_op jit(solution)/shard_map/ppermute | solution.py:25
  61.9 11.3 %collective-permute-start.5 = (f32[1,4,1,8,128]{4,3,2,1,0:T(8,128)S(1)}, f32[1,4,1,8,128]{4,3,2,1,0:T(8,128)S(1)}, u32[]{:S(2)}, u32[]{:S(2)}) collective-permute-start(f32[1,4,1,8,128]{4,3,2,1,0:T(8,128)S(1)} %get-tuple-element.76), channel_id=1, source_target_pairs={{1,0},{2,1},{3,2},{4,3},{5,4},{6,5},{7,6},{8,7},{9,8},{10,9},{11,1... | collective-permute-start | bytes 49160 | tf_op jit(solution)/shard_map/ppermute | solution.py:26
  73.8 10.7 %collective-permute-start.8 = (f32[1,4,1,8,128]{4,3,2,1,0:T(8,128)S(1)}, f32[1,4,1,8,128]{4,3,2,1,0:T(8,128)S(1)}, u32[]{:S(2)}, u32[]{:S(2)}) collective-permute-start(f32[1,4,1,8,128]{4,3,2,1,0:T(8,128)S(1)} %get-tuple-element.73), channel_id=1, source_target_pairs={{0,1},{1,2},{2,3},{3,4},{4,5},{5,6},{6,7},{7,8},{8,9},{9,10},{10,1... | collective-permute-start | bytes 49160 | tf_op jit(solution)/shard_map/ppermute | solution.py:25
  78.4 9.5 %collective-permute-start.7 = (f32[1,4,1,8,128]{4,3,2,1,0:T(8,128)S(1)}, f32[1,4,1,8,128]{4,3,2,1,0:T(8,128)S(1)}, u32[]{:S(2)}, u32[]{:S(2)}) collective-permute-start(f32[1,4,1,8,128]{4,3,2,1,0:T(8,128)S(1)} %get-tuple-element.74), channel_id=1, source_target_pairs={{1,0},{2,1},{3,2},{4,3},{5,4},{6,5},{7,6},{8,7},{9,8},{10,9},{11,1... | collective-permute-start | bytes 49160 | tf_op jit(solution)/shard_map/ppermute | solution.py:26
  108.1 21.6 %copy-start.4 = (f32[5,4,3,4,64]{4,3,2,1,0:T(4,128)}, f32[5,4,3,4,64]{4,3,2,1,0:T(4,128)S(1)}, u32[]{:S(2)}) copy-start(f32[5,4,3,4,64]{4,3,2,1,0:T(4,128)S(1)} %broadcast_multiply_fusion.4) | copy-start | bytes 184324
  108.1 21.5 %collective-permute-start.14 = (f32[3,4,1,4,64]{4,3,2,1,0:T(4,128)S(1)}, f32[3,4,1,4,64]{4,3,2,1,0:T(4,128)S(1)}, u32[]{:S(2)}, u32[]{:S(2)}) collective-permute-start(f32[3,4,1,4,64]{4,3,2,1,0:T(4,128)S(1)} %get-tuple-element.60), channel_id=1, source_target_pairs={{0,1},{1,2},{2,3},{3,4},{4,5},{5,6},{6,7},{7,8},{8,9},{9,10},{10,1... | collective-permute-start | bytes 36872 | tf_op jit(solution)/shard_map/ppermute | solution.py:25
  110.5 19.2 %collective-permute-start.13 = (f32[3,4,1,4,64]{4,3,2,1,0:T(4,128)S(1)}, f32[3,4,1,4,64]{4,3,2,1,0:T(4,128)S(1)}, u32[]{:S(2)}, u32[]{:S(2)}) collective-permute-start(f32[3,4,1,4,64]{4,3,2,1,0:T(4,128)S(1)} %get-tuple-element.61), channel_id=1, source_target_pairs={{1,0},{2,1},{3,2},{4,3},{5,4},{6,5},{7,6},{8,7},{9,8},{10,9},{11,1... | collective-permute-start | bytes 36872 | tf_op jit(solution)/shard_map/ppermute | solution.py:26
  118.8 12.0 %collective-permute-start.10 = (f32[1,4,1,8,128]{4,3,2,1,0:T(8,128)S(1)}, f32[1,4,1,8,128]{4,3,2,1,0:T(8,128)S(1)}, u32[]{:S(2)}, u32[]{:S(2)}) collective-permute-start(f32[1,4,1,8,128]{4,3,2,1,0:T(8,128)S(1)} %get-tuple-element.71), channel_id=1, source_target_pairs={{0,1},{1,2},{2,3},{3,4},{4,5},{5,6},{6,7},{7,8},{8,9},{9,10},{10,1... | collective-permute-start | bytes 49160 | tf_op jit(solution)/shard_map/ppermute | solution.py:25
  120.8 10.2 %collective-permute-start.9 = (f32[1,4,1,8,128]{4,3,2,1,0:T(8,128)S(1)}, f32[1,4,1,8,128]{4,3,2,1,0:T(8,128)S(1)}, u32[]{:S(2)}, u32[]{:S(2)}) collective-permute-start(f32[1,4,1,8,128]{4,3,2,1,0:T(8,128)S(1)} %get-tuple-element.72), channel_id=1, source_target_pairs={{1,0},{2,1},{3,2},{4,3},{5,4},{6,5},{7,6},{8,7},{9,8},{10,9},{11,1... | collective-permute-start | bytes 49160 | tf_op jit(solution)/shard_map/ppermute | solution.py:26
  161.6 16.4 %copy-start.2 = (f32[4,3,4,64]{0,3,2,1:T(8,128)S(1)}, f32[4,3,4,64]{0,3,2,1:T(8,128)}, u32[]{:S(2)}) copy-start(f32[4,3,4,64]{0,3,2,1:T(8,128)} %broadcast_multiply_fusion) | copy-start | bytes 36868
  163.4 14.7 %copy-start.3 = (f32[4,3,4,64]{0,3,2,1:T(8,128)S(1)}, f32[4,3,4,64]{0,3,2,1:T(8,128)}, u32[]{:S(2)}) copy-start(f32[4,3,4,64]{0,3,2,1:T(8,128)} %broadcast_multiply_fusion.1) | copy-start | bytes 36868
  164.3 11.7 %copy-start.6 = (f32[1,4,3,4,64]{4,3,2,1,0:T(4,128)}, f32[1,4,3,4,64]{4,3,2,1,0:T(4,128)S(1)}, u32[]{:S(2)}) copy-start(f32[1,4,3,4,64]{4,3,2,1,0:T(4,128)S(1)} %get-tuple-element.27) | copy-start | bytes 36868
  164.9 14.6 %collective-permute-start.12 = (f32[1,4,1,4,64]{4,3,2,1,0:T(4,128)}, f32[1,4,1,4,64]{4,3,2,1,0:T(4,128)}, u32[]{:S(2)}, u32[]{:S(2)}) collective-permute-start(f32[1,4,1,4,64]{4,3,2,1,0:T(4,128)} %get-tuple-element.83), channel_id=1, source_target_pairs={{0,1},{1,2},{2,3},{3,4},{4,5},{5,6},{6,7},{7,8},{8,9},{9,10},{10,1... | collective-permute-start | bytes 12296 | tf_op jit(solution)/shard_map/ppermute | solution.py:25
  170.3 9.8 %collective-permute-start.11 = (f32[1,4,1,4,64]{4,3,2,1,0:T(4,128)}, f32[1,4,1,4,64]{4,3,2,1,0:T(4,128)}, u32[]{:S(2)}, u32[]{:S(2)}) collective-permute-start(f32[1,4,1,4,64]{4,3,2,1,0:T(4,128)} %get-tuple-element.84), channel_id=1, source_target_pairs={{1,0},{2,1},{3,2},{4,3},{5,4},{6,5},{7,6},{8,7},{9,8},{10,9},{11,1... | collective-permute-start | bytes 12296 | tf_op jit(solution)/shard_map/ppermute | solution.py:26
  176.8 3.2 %copy-start.7 = (f32[1,4,3,4,64]{4,3,2,1,0:T(4,128)S(1)}, f32[1,4,3,4,64]{4,3,2,1,0:T(4,128)}, u32[]{:S(2)}) copy-start(f32[1,4,3,4,64]{4,3,2,1,0:T(4,128)} %copy-done.6) | copy-start | bytes 36868
  176.8 6.3 %copy-start.5 = (f32[5,4,3,4,64]{4,3,2,1,0:T(4,128)S(1)}, f32[5,4,3,4,64]{4,3,2,1,0:T(4,128)}, u32[]{:S(2)}) copy-start(f32[5,4,3,4,64]{4,3,2,1,0:T(4,128)} %copy-done.4) | copy-start | bytes 184324
  176.9 6.3 %copy-start.10 = (f32[3,4,3,4,64]{4,3,2,1,0:T(4,128)S(1)}, f32[3,4,3,4,64]{4,3,2,1,0:T(4,128)}, u32[]{:S(2)}) copy-start(f32[3,4,3,4,64]{4,3,2,1,0:T(4,128)} %pad_maximum_fusion.7) | copy-start | bytes 110596
  183.2 12.7 %collective-permute-start.16 = (f32[1,4,1,4,64]{4,3,2,1,0:T(4,128)S(1)}, f32[1,4,1,4,64]{4,3,2,1,0:T(4,128)S(1)}, u32[]{:S(2)}, u32[]{:S(2)}) collective-permute-start(f32[1,4,1,4,64]{4,3,2,1,0:T(4,128)S(1)} %get-tuple-element.81), channel_id=1, source_target_pairs={{0,1},{1,2},{2,3},{3,4},{4,5},{5,6},{6,7},{7,8},{8,9},{9,10},{10,1... | collective-permute-start | bytes 12296 | tf_op jit(solution)/shard_map/ppermute | solution.py:25
  190.4 9.5 %collective-permute-start.15 = (f32[1,4,1,4,64]{4,3,2,1,0:T(4,128)S(1)}, f32[1,4,1,4,64]{4,3,2,1,0:T(4,128)S(1)}, u32[]{:S(2)}, u32[]{:S(2)}) collective-permute-start(f32[1,4,1,4,64]{4,3,2,1,0:T(4,128)S(1)} %get-tuple-element.82), channel_id=1, source_target_pairs={{1,0},{2,1},{3,2},{4,3},{5,4},{6,5},{7,6},{8,7},{9,8},{10,9},{11,1... | collective-permute-start | bytes 12296 | tf_op jit(solution)/shard_map/ppermute | solution.py:26
  200.3 12.7 %collective-permute-start.18 = (f32[1,4,1,4,64]{4,3,2,1,0:T(4,128)S(1)}, f32[1,4,1,4,64]{4,3,2,1,0:T(4,128)S(1)}, u32[]{:S(2)}, u32[]{:S(2)}) collective-permute-start(f32[1,4,1,4,64]{4,3,2,1,0:T(4,128)S(1)} %get-tuple-element.79), channel_id=1, source_target_pairs={{0,1},{1,2},{2,3},{3,4},{4,5},{5,6},{6,7},{7,8},{8,9},{9,10},{10,1... | collective-permute-start | bytes 12296 | tf_op jit(solution)/shard_map/ppermute | solution.py:25
  207.1 9.5 %collective-permute-start.17 = (f32[1,4,1,4,64]{4,3,2,1,0:T(4,128)S(1)}, f32[1,4,1,4,64]{4,3,2,1,0:T(4,128)S(1)}, u32[]{:S(2)}, u32[]{:S(2)}) collective-permute-start(f32[1,4,1,4,64]{4,3,2,1,0:T(4,128)S(1)} %get-tuple-element.80), channel_id=1, source_target_pairs={{1,0},{2,1},{3,2},{4,3},{5,4},{6,5},{7,6},{8,7},{9,8},{10,9},{11,1... | collective-permute-start | bytes 12296 | tf_op jit(solution)/shard_map/ppermute | solution.py:26
  212.9 14.6 %copy-start.9 = (f32[4,6,8,128]{3,2,1,0:T(8,128)S(1)}, f32[4,6,8,128]{3,2,1,0:T(8,128)}, u32[]{:S(2)}) copy-start(f32[4,6,8,128]{3,2,1,0:T(8,128)} %param.5) | copy-start | bytes 294916
  218.9 8.6 %collective-permute-start.19 = (f32[1,4,6,8,128]{4,3,2,1,0:T(8,128)S(1)}, f32[1,4,6,8,128]{4,3,2,1,0:T(8,128)S(1)}, u32[]{:S(2)}, u32[]{:S(2)}) collective-permute-start(f32[1,4,6,8,128]{4,3,2,1,0:T(8,128)S(1)} %get-tuple-element.21), channel_id=1, source_target_pairs={{0,16},{16,32},{32,48},{48,64},{64,80},{80,96},{96,112},{112,128},... | collective-permute-start | bytes 294920 | tf_op jit(solution)/shard_map/ppermute | solution.py:15
where the time goes:
time: 230 us; the launch traced here: 228 us
  starting transfers between devices  104 us (45%)
  other arithmetic  54.4 us (24%)
  waiting for transfers between devices  38.8 us (17%)
  local copies, waits for them, and re-layouts  29.3 us (13%)
    ppermute x9, starting transfers between devices, padded_2(): before = lax.ppermute(last, axis, up)  50.7 us
    ppermute x9, starting transfers between devices, padded_2(): after = lax.ppermute(first, axis, down)  49.6 us
    reduce_sum x7, other arithmetic, restrict(): return jnp.mean(source.reshape(new_shape), axis=(-5, -3, -1))  28.5 us
    ppermute x9, waiting for transfers between devices, padded_2(): after = lax.ppermute(first, axis, down)  24.8 us
    ppermute x2, waiting for transfers between devices, from_behind(): lax.ppermute(value, axis, [(source, source + steps) for source in range(f...  13.4 us
    add x4, local copies, waits for them, and re-layouts, spread_sum(): total = total + table_row[position] * images[position:position + 1]  7.56 us
    concatenate x1, local copies, waits for them, and re-layouts, fine_sweep(): return (jnp.concatenate(values, axis=0), jnp.concatenate(images, axis=0))  6.8 us
    div x6, other arithmetic, restrict(): return jnp.mean(source.reshape(new_shape), axis=(-5, -3, -1))  6.46 us
  transfers between devices with their start and end apart: 20, of which 10 were waited for; matrix products, arithmetic and copies ran while one was open for 7% of the time, Pallas kernels for 0%

commit v1 on v0

v1 whole, which is shorter than its diff:
```python
import functools
import math

import jax
import jax.numpy as jnp
from jax import lax
from jax.experimental import pallas as pl
from jax.experimental.pallas import tpu as pltpu
from jax.sharding import PartitionSpec as P

MESH = pl.DeviceIdType.MESH
slice_step = 0.4
LAYERS = 6
EXT = 12
FIELD = 4


def node_tables():
    root_gap = math.sqrt(3.0 / 7.0)
    points = [0.0, (1.0 - root_gap) / 2.0, 0.5, (1.0 + root_gap) / 2.0, 1.0]
    polys = []
    for node in range(5):
        coeffs = [1.0]
        for other in range(5):
            if other != node:
                denom = points[node] - points[other]
                grown = [0.0] * (len(coeffs) + 1)
                for power in range(len(coeffs)):
                    grown[power + 1] += coeffs[power] / denom
                    grown[power] -= points[other] * coeffs[power] / denom
                coeffs = grown
        polys.append(coeffs)
    integral = []
    for column in range(4):
        lower = points[column]
        upper = points[column + 1]
        table_row = []
        for node in range(5):
            total = 0.0
            for power in range(5):
                total += (
                    polys[node][power] * (upper ** (power + 1) - lower ** (power + 1)) / (power + 1)
                )
            table_row.append(total * slice_step)
        integral.append(table_row)
    widths = [(points[column + 1] - points[column]) * slice_step for column in range(4)]
    return (integral, widths)


def positions(shape, axis):
    return lax.broadcasted_iota(jnp.int32, shape, axis)


def at(value, axis, step):
    size = value.shape[axis]
    moved = pltpu.roll(value, (-step) % size, axis)
    where = positions(value.shape, axis)
    inside = where < size - step if step > 0 else where >= -step
    return jnp.where(inside, moved, 0.0)


def operator(q, stiff, fluid, grad, step):
    out = [None] * 4
    diverge = None
    for k in (3, 0, 1, 2):
        center, below, above = q[k][1:-1], q[k][:-2], q[k][2:]
        xp, xm = at(center, 1, step), at(center, 1, -step)
        yp, ym = at(center, 2, step), at(center, 2, -step)
        laplace = ((xp + xm) + (yp + ym)) + (above + below) - 6.0 * center
        if k == 3:
            flow = fluid * laplace
            grads = [grad * (above - below), grad * (xp - xm), grad * (yp - ym)]
        else:
            out[k] = stiff * laplace - grads[k]
            part = (above - below, xp - xm, yp - ym)[k]
            diverge = part if diverge is None else diverge + part
    out[3] = flow - grad * diverge
    return out


def from_below(q, stiff, fluid, grad):
    return [stiff * q[0] + grad * q[3], stiff * q[1], stiff * q[2], fluid * q[3] + grad * q[0]]


def from_above(q, stiff, fluid, grad):
    return [stiff * q[0] - grad * q[3], stiff * q[1], stiff * q[2], fluid * q[3] - grad * q[0]]


def even(shape, axis):
    return positions(shape, axis) % 2 == 0


def pair_sums(a, b, axis):
    size = a.shape[axis]
    is_even = even(a.shape, axis)
    kept, other = jnp.where(is_even, a, b), jnp.where(is_even, b, a)
    return kept + jnp.where(is_even, pltpu.roll(other, size - 1, axis), pltpu.roll(other, 1, axis))


def means(q):
    return 0.125 * pair_sums(pair_sums(q[0], q[1], 2), pair_sums(q[2], q[3], 2), 1)


def layer_pairs(v):
    return jnp.concatenate([v[2 * i : 2 * i + 1] + v[2 * i + 1 : 2 * i + 2] for i in range(3)], axis=0)


def woven(q):
    shape = q[0].shape
    ye, xe = even(shape, 2), even(shape, 1)
    return jnp.where(xe, jnp.where(ye, q[0], q[1]), jnp.where(ye, q[2], q[3]))


def spread(p):
    ye, xe = even(p.shape, 2), even(p.shape, 1)
    a = jnp.where(ye, p, pltpu.roll(p, 1, 2))
    b = jnp.where(ye, pltpu.roll(p, 127, 2), p)
    return [
        jnp.where(xe, a, pltpu.roll(a, 1, 1)),
        jnp.where(xe, b, pltpu.roll(b, 1, 1)),
        jnp.where(xe, pltpu.roll(a, 7, 1), a),
        jnp.where(xe, pltpu.roll(b, 7, 1), b),
    ]


def twice(v):
    return jnp.concatenate([v[i // 2 : i // 2 + 1] for i in range(LAYERS)], axis=0)


def ends(v, low, high):
    return jnp.concatenate([v[:1] + low, v[1:-1], v[-1:] + high], axis=0)


def padded(v):
    zero = jnp.zeros_like(v[:1])
    return jnp.concatenate([zero, v, zero], axis=0)


def kernel(
    counts,
    old_hbm,
    init_hbm,
    shear_hbm,
    mobil_hbm,
    new_hbm,
    next_hbm,
    old,
    init,
    coef,
    coef_in,
    u,
    fu,
    start_in,
    primed,
    faces,
    node,
    halo,
    face_out,
    face_in,
    error,
    coarse_out,
    coarse_in,
    last_in,
    end_out,
    end_in,
    result,
    local_sem,
    write_sem,
    tm_send,
    tm_recv,
    coef_send,
    coef_recv,
    face_send,
    face_recv,
    coarse_send,
    coarse_recv,
):
    integral, widths = node_tables()
    table = [[integral[m][j] - (widths[m] if j == m else 0.0) for j in range(5)] for m in range(4)]
    slices, slabs = counts
    t, s = lax.axis_index("tm"), lax.axis_index("space")
    before, after = (lax.rem(t + slices - 1, slices), s), (lax.rem(t + 1, slices), s)
    below, above = (t, lax.rem(s + slabs - 1, slabs)), (t, lax.rem(s + 1, slabs))
    has_below, has_above, is_first = s > 0, s < slabs - 1, t == 0
    exists = (has_below, has_above)

    barrier = pltpu.get_barrier_semaphore()
    for device in (before, below, above):
        pl.semaphore_signal(barrier, inc=1, device_id=device, device_id_type=MESH)

    loads = [
        pltpu.make_async_copy(old_hbm.at[0], old, local_sem.at[0]),
        pltpu.make_async_copy(shear_hbm, coef.at[0, pl.ds(3, LAYERS)], local_sem.at[1]),
        pltpu.make_async_copy(mobil_hbm, coef.at[1, pl.ds(3, LAYERS)], local_sem.at[2]),
        pltpu.make_async_copy(init_hbm, init, local_sem.at[3]),
    ]
    for load in loads:
        load.start()
    for load in loads:
        load.wait()

    stiff, fluid = coef[0, 3 : 3 + LAYERS], coef[1, 3 : 3 + LAYERS]

    for m in range(4):
        for k in range(FIELD):
            total = table[m][0] * old[0, k]
            for j in range(1, 5):
                total = total + table[m][j] * old[j, k]
            u[m, k] = total
    for m in range(4):
        images = operator([padded(u[m, k]) for k in range(FIELD)], stiff, fluid, 0.25, 1)
        for k in range(FIELD):
            fu[m, k] = images[k]

    pl.semaphore_wait(barrier, 3)

    def remote(src, dst, send, recv, device):
        return pltpu.make_async_remote_copy(
            src_ref=src, dst_ref=dst, send_sem=send, recv_sem=recv, device_id=device, device_id_type=MESH
        )

    start_copy = remote(old.at[4], start_in, tm_send.at[0], tm_recv.at[0], after)
    start_copy.start()
    coef_copies = [
        remote(coef.at[:, pl.ds(3, 3)], coef_in.at[1], coef_send.at[0], coef_recv.at[1], below),
        remote(coef.at[:, pl.ds(6, 3)], coef_in.at[0], coef_send.at[1], coef_recv.at[0], above),
    ]
    for copy in coef_copies:
        copy.start()

    start_copy.wait_recv()
    for k in range(FIELD):
        first = jnp.where(is_first, init[k], start_in[k])
        node[0, k] = first
        primed[k] = padded(first)
    writes = [pltpu.make_async_copy(node.at[0], new_hbm.at[0, 0], write_sem.at[0])]
    writes[0].start()

    face_copies = []
    for m in range(5):
        for side, layer in ((0, 0), (1, LAYERS - 1)):
            for k in range(FIELD):
                face = primed[k, layer + 1]
                faces[side, m, k] = face
                if m < 4:
                    face_out[side, m, k] = widths[m] * face + u[m, k, layer]
        if m == 4:
            break
        for side, device in ((0, below), (1, above)):
            copy = remote(
                face_out.at[side, m],
                face_in.at[1 - side, m],
                face_send.at[side, m],
                face_recv.at[1 - side, m],
                device,
            )
            copy.start()
            face_copies.append(copy)
        images = operator([primed[k] for k in range(FIELD)], stiff, fluid, 0.25, 1)
        for k in range(FIELD):
            moved = primed[k, 1 : 1 + LAYERS] + widths[m] * images[k] + fu[m, k]
            primed[k, 1 : 1 + LAYERS] = moved
            if m == 0:
                node[1, k] = moved
                error[0, k] = images[k]

    for copy in coef_copies:
        copy.wait_recv()
    for array in range(2):
        coef[array, 0:3] = jnp.where(has_below, coef_in[0, array], 0.0)
        coef[array, 9:12] = jnp.where(has_above, coef_in[1, array], 0.0)
    gradients = [jnp.where(exists[side], 0.25, 0.0) for side in range(2)]

    def across(q, side):
        layer = (2, 9)[side]
        reach = (from_above, from_below)[side]
        return reach(q, coef[0, layer : layer + 1], coef[1, layer : layer + 1], gradients[side])

    for side in range(2):
        layer = (0, LAYERS - 1)[side]
        for m in range(4):
            z = []
            for k in range(FIELD):
                total = table[m][0] * faces[side, 0, k]
                for j in range(1, 5):
                    total = total + table[m][j] * faces[side, j, k]
                z.append((total - u[m, k, layer])[None])
            face_out[side, 4, m] = means(across(z, side))[0]
    for side, device in ((0, below), (1, above)):
        copy = remote(
            face_out.at[side, 4],
            face_in.at[1 - side, 4],
            face_send.at[side, 4],
            face_recv.at[1 - side, 4],
            device,
        )
        copy.start()
        face_copies.append(copy)

    def inflow(side, m):
        layer = (3, 8)[side]
        q = [jnp.where(exists[side], face_in[side, m, k], 0.0)[None] for k in range(FIELD)]
        reach = (from_below, from_above)[side]
        return reach(q, coef[0, layer : layer + 1], coef[1, layer : layer + 1], 0.25)

    def edge(m, side):
        return [u[m, k, (0, LAYERS - 1)[side]][None] for k in range(FIELD)]

    for side in range(2):
        face_copies[side].wait_recv()
    low, high = inflow(0, 0), inflow(1, 0)
    zero = jnp.zeros((2, 8, 128), jnp.float32)
    out_low = across([face_out[0, 0, k][None] for k in range(FIELD)], 0)
    out_high = across([face_out[1, 0, k][None] for k in range(FIELD)], 1)
    for k in range(FIELD):
        node[1, k] = ends(node[1, k], low[k], high[k])
        halo[0, k] = jnp.concatenate([zero, out_low[k]], axis=0)
        halo[1, k] = jnp.concatenate([out_high[k], zero], axis=0)

    sums = [means([layer_pairs(error[0, k]) for k in range(FIELD)])]
    grad = jnp.concatenate(
        [
            jnp.full((3, 8, 128), 1.0, jnp.float32) * gradients[0],
            jnp.full((LAYERS, 8, 128), 0.25, jnp.float32),
            jnp.full((3, 8, 128), 1.0, jnp.float32) * gradients[1],
        ],
        axis=0,
    )
    for m in range(1, 5):
        reach = (0, 2, 3, 1, 0)[m]
        own = slice(reach, reach + LAYERS)
        lo, hi = 3 - reach, 9 + reach
        q = []
        for k in range(FIELD):
            if reach == 3:
                whole = padded(jnp.concatenate([halo[0, k], node[m, k], halo[1, k]], axis=0))
            else:
                whole = jnp.concatenate(
                    [halo[0, k, 2 - reach :], node[m, k], halo[1, k, : reach + 1]], axis=0
                )
            q.append(whole)
        images = operator(q, coef[0, lo:hi], coef[1, lo:hi], grad[lo:hi], 1)
        sums.append(means([layer_pairs(images[k][own]) for k in range(FIELD)]))
        if m == 4:
            break
        for side in range(2):
            face_copies[2 * m + side].wait_recv()
        low, high = inflow(0, m), inflow(1, m)
        out_low, out_high = across(edge(m, 0), 0), across(edge(m, 1), 1)
        for k in range(FIELD):
            moved = node[m, k] + widths[m] * images[k][own] + fu[m, k]
            node[m + 1, k] = ends(moved, low[k], high[k])
            inner = halo[0, k, 3 - reach :] + widths[m] * images[k][:reach]
            halo[0, k, 3 - reach :] = jnp.concatenate([inner[:-1], inner[-1:] + out_low[k]], axis=0) if reach > 1 else inner + out_low[k]
            inner = halo[1, k, :reach] + widths[m] * images[k][reach + LAYERS :]
            halo[1, k, :reach] = jnp.concatenate([inner[:1] + out_high[k], inner[1:]], axis=0) if reach > 1 else inner + out_high[k]

    last_copy = remote(node.at[4], last_in, tm_send.at[1], tm_recv.at[1], after)
    last_copy.start()

    for side in range(2):
        face_copies[8 + side].wait_recv()
    for m in range(4):
        total = table[m][0] * sums[0]
        for j in range(1, 5):
            total = total + table[m][j] * sums[j]
        total = total - means([layer_pairs(fu[m, k]) for k in range(FIELD)])
        total = ends(
            total,
            jnp.where(has_below, face_in[0, 4, m], 0.0)[None],
            jnp.where(has_above, face_in[1, 4, m], 0.0)[None],
        )
        spread_out = spread(total)
        for k in range(FIELD):
            error[m, k, 0:3] = spread_out[k]

    def coarse_coef(lo, pairs):
        both = [
            jnp.concatenate([coef[a, lo + 2 * i : lo + 2 * i + 1] + coef[a, lo + 2 * i + 1 : lo + 2 * i + 2] for i in range(pairs)], axis=0)
            for a in range(2)
        ]
        pieces = spread(means([both[0], both[0], both[1], both[1]]))
        return 0.25 * pieces[0], 0.25 * pieces[2]

    coarse_stiff, coarse_fluid = coarse_coef(1, 5)
    weight = 0.5 * grad[2:10]
    coarse_grad = jnp.concatenate([weight[0:1], weight[1:4], weight[7:8]], axis=0)
    own_stiff, own_fluid = coarse_stiff[1:4], coarse_fluid[1:4]

    def send_coarse(m, d):
        for side, layer in ((0, 0), (1, 2)):
            coarse_out[side, m] = woven([d[k][layer : layer + 1] for k in range(FIELD)])[0]

    d1 = [error[0, k, 0:3] for k in range(FIELD)]
    send_coarse(0, d1)
    f1 = operator([padded(v) for v in d1], own_stiff, own_fluid, 0.125, 2)
    d2 = [d1[k] + widths[1] * f1[k] + error[1, k, 0:3] for k in range(FIELD)]
    send_coarse(1, d2)
    f2 = operator([padded(v) for v in d2], own_stiff, own_fluid, 0.125, 2)
    d3 = [d2[k] + widths[2] * f2[k] + error[2, k, 0:3] for k in range(FIELD)]
    send_coarse(2, d3)
    coarse_copies = []
    for side, device in ((0, below), (1, above)):
        copy = remote(
            coarse_out.at[side],
            coarse_in.at[1 - side],
            coarse_send.at[side],
            coarse_recv.at[1 - side],
            device,
        )
        copy.start()
        coarse_copies.append(copy)

    def finish(m, d):
        for k in range(FIELD):
            result[m - 1, k] = node[m, k] + twice(d[k])
        write = pltpu.make_async_copy(result.at[m - 1], new_hbm.at[0, m], write_sem.at[m])
        write.start()
        writes.append(write)

    finish(1, d1)

    def coarse_across(q, side):
        layer = (0, 4)[side]
        reach = (from_above, from_below)[side]
        part = slice(layer, layer + 1)
        return reach(q, coarse_stiff[part], coarse_fluid[part], coarse_grad[part])

    halo_low = [widths[1] * v for v in coarse_across([v[0:1] for v in d1], 0)]
    halo_high = [widths[1] * v for v in coarse_across([v[2:3] for v in d1], 1)]

    for copy in coarse_copies:
        copy.wait_recv()
    coming = [
        [spread(jnp.where(exists[side], coarse_in[side, m], 0.0)[None]) for m in range(3)] for side in range(2)
    ]

    def coarse_inflow(m):
        low = from_below(coming[0][m], own_stiff[0:1], own_fluid[0:1], 0.125)
        high = from_above(coming[1][m], own_stiff[2:3], own_fluid[2:3], 0.125)
        return low, high

    low, high = coarse_inflow(0)
    d2 = [ends(d2[k], widths[1] * low[k], widths[1] * high[k]) for k in range(FIELD)]
    finish(2, d2)
    low, high = coarse_inflow(1)
    q = [padded(jnp.concatenate([halo_low[k], d2[k], halo_high[k]], axis=0)) for k in range(FIELD)]
    images = operator(q, coarse_stiff, coarse_fluid, coarse_grad, 2)
    d3 = [
        d2[k] + widths[2] * ends(images[k][1:4], low[k], high[k]) + error[2, k, 0:3] for k in range(FIELD)
    ]
    finish(3, d3)
    halo_low = [halo_low[k] + widths[2] * images[k][0:1] + coming[0][2][k] for k in range(FIELD)]
    halo_high = [halo_high[k] + widths[2] * images[k][4:5] + coming[1][2][k] for k in range(FIELD)]
    q = [jnp.concatenate([halo_low[k], d3[k], halo_high[k]], axis=0) for k in range(FIELD)]
    images = operator(q, own_stiff, own_fluid, 0.125, 2)
    d4 = [d3[k] + widths[3] * images[k] + error[3, k, 0:3] for k in range(FIELD)]
    end_out[...] = woven(d4)
    end_copy = remote(end_out, end_in, tm_send.at[2], tm_recv.at[2], after)
    end_copy.start()
    finish(4, d4)

    last_copy.wait_recv()
    end_copy.wait_recv()
    d4 = spread(end_in[...])
    for k in range(FIELD):
        start_in[k] = jnp.where(is_first, init[k], last_in[k] + twice(d4[k]))
    write = pltpu.make_async_copy(start_in, next_hbm.at[0], write_sem.at[5])
    write.start()
    writes.append(write)

    for copy in [start_copy, last_copy, end_copy] + coef_copies + face_copies + coarse_copies:
        copy.wait_send()
    for write in writes:
        write.wait()


def on_device(counts, old_nodes, initial, shear_modulus, mobility):
    def vmem(*shape):
        return pltpu.VMEM(shape + (8, 128), jnp.float32)

    dma = pltpu.SemaphoreType.DMA
    return pl.pallas_call(
        functools.partial(kernel, counts),
        out_shape=(
            jax.ShapeDtypeStruct((1, 5, FIELD, LAYERS, 8, 128), jnp.float32),
            jax.ShapeDtypeStruct((1, FIELD, LAYERS, 8, 128), jnp.float32),
        ),
        in_specs=[pl.BlockSpec(memory_space=pl.ANY)] * 4,
        out_specs=(pl.BlockSpec(memory_space=pl.ANY),) * 2,
        scratch_shapes=[
            vmem(5, FIELD, LAYERS),
            vmem(FIELD, LAYERS),
            vmem(2, EXT),
            vmem(2, 2, 3),
            vmem(4, FIELD, LAYERS),
            vmem(4, FIELD, LAYERS),
            vmem(FIELD, LAYERS),
            vmem(FIELD, LAYERS + 2),
            vmem(2, 5, FIELD),
            vmem(5, FIELD, LAYERS),
            vmem(2, FIELD, 3),
            vmem(2, 5, FIELD),
            vmem(2, 5, FIELD),
            vmem(4, FIELD, LAYERS),
            vmem(2, 3),
            vmem(2, 3),
            vmem(FIELD, LAYERS),
            vmem(3),
            vmem(3),
            vmem(4, FIELD, LAYERS),
            dma((4,)),
            dma((6,)),
            dma((3,)),
            dma((3,)),
            dma((2,)),
            dma((2,)),
            dma((2, 5)),
            dma((2, 5)),
            dma((2,)),
            dma((2,)),
        ],
        compiler_params=pltpu.CompilerParams(
            collective_id=0, has_side_effects=True, vmem_limit_bytes=32 * 1024 * 1024
        ),
    )(old_nodes, initial, shear_modulus, mobility)


def solution(mesh):
    counts = (mesh.shape["tm"], mesh.shape["space"])
    return jax.shard_map(
        functools.partial(on_device, counts),
        mesh=mesh,
        in_specs=(
            P("tm", None, None, "space", None, None),
            P(None, "space", None, None),
            P("space", None, None),
            P("space", None, None),
        ),
        out_specs=(P("tm", None, None, "space", None, None), P("tm", None, "space", None, None)),
        check_vma=False,
    )
```

time: 230 us -> 44.5 us (0.19)
  the two profiles are of different devices: /device:TPU:20 before, /device:TPU:1 now
where the time goes in v1:
time: 44.5 us; the launch traced here: 44.1 us
  Pallas kernels  38.7 us (87%)
  local copies, waits for them, and re-layouts  4.81 us (11%)
  between operations  0.65 us (1%)
    pallas_call x1, Pallas kernels, on_device(): pl.pallas_call(functools.partial(kernel, counts), out_shape=(jax.ShapeDty...  38.7 us
    unnamed x10, local copies, waits for them, and re-layouts  4.81 us

profile of v1, /device:TPU:1, one launch (start us, length us, event | category | flops | bytes accessed | tf_op | source)
XLA Modules:
  0.0 44.1 jit_solution(12790562319297092973)
XLA Ops:
  0.6 0.0 copy-start
  0.6 1.0 %copy-done = f32[1,5,4,6,8,128]{5,4,3,2,1,0:T(8,128)S(1)} copy-done((f32[1,5,4,6,8,128]{5,4,3,2,1,0:T(8,128)S(1)}, f32[1,5,4,6,8,128]{5,4,3,2,1,0:T(8,128)}, u32[]{:S(2)}) %copy-start) | copy-done | bytes 491544
  1.7 0.0 copy-start.1
  1.7 0.9 %copy-done.1 = f32[4,6,8,128]{3,2,1,0:T(8,128)S(1)} copy-done((f32[4,6,8,128]{3,2,1,0:T(8,128)S(1)}, f32[4,6,8,128]{3,2,1,0:T(8,128)}, u32[]{:S(2)}) %copy-start.1) | copy-done | bytes 98328
  2.6 0.0 copy-start.2
  2.6 0.7 %copy-done.2 = f32[6,8,128]{2,1,0:T(8,128)S(1)} copy-done((f32[6,8,128]{2,1,0:T(8,128)S(1)}, f32[6,8,128]{2,1,0:T(8,128)}, u32[]{:S(2)}) %copy-start.2) | copy-done | bytes 24600
  3.3 0.0 copy-start.3
  3.3 0.7 %copy-done.3 = f32[6,8,128]{2,1,0:T(8,128)S(1)} copy-done((f32[6,8,128]{2,1,0:T(8,128)S(1)}, f32[6,8,128]{2,1,0:T(8,128)}, u32[]{:S(2)}) %copy-start.3) | copy-done | bytes 24600
  4.0 38.7 %shard_map.59 = (f32[1,5,4,6,8,128]{5,4,3,2,1,0:T(8,128)S(1)}, f32[1,4,6,8,128]{4,3,2,1,0:T(8,128)S(1)}) custom-call(f32[1,5,4,6,8,128]{5,4,3,2,1,0:T(8,128)S(1)} %copy-done, f32[4,6,8,128]{3,2,1,0:T(8,128)S(1)} %copy-done.1, f32[6,8,128]{2,1,0:T(8,128)S(1)} %copy-done.2, f32[6,8,128]{2,1,0:T(8,128)S(1)} %copy-done.3), custom_call_target="tpu_custom_call" | custom-call | tf_op jit(solution)/shard_map/pallas_call | solution.py:483
  42.7 0.8 %copy.8 = f32[1,5,4,6,8,128]{5,4,3,2,1,0:T(8,128)} copy(f32[1,5,4,6,8,128]{5,4,3,2,1,0:T(8,128)S(1)} %get-tuple-element.4) | data formatting | bytes 983040
  43.5 0.6 %copy.9 = f32[1,4,6,8,128]{4,3,2,1,0:T(8,128)} copy(f32[1,4,6,8,128]{4,3,2,1,0:T(8,128)S(1)} %get-tuple-element.5) | data formatting | bytes 196608
Async XLA Ops:
  0.6 1.0 %copy-start = (f32[1,5,4,6,8,128]{5,4,3,2,1,0:T(8,128)S(1)}, f32[1,5,4,6,8,128]{5,4,3,2,1,0:T(8,128)}, u32[]{:S(2)}) copy-start(f32[1,5,4,6,8,128]{5,4,3,2,1,0:T(8,128)} %old_hbm.1) | copy-start | bytes 1474564
  1.7 0.9 %copy-start.1 = (f32[4,6,8,128]{3,2,1,0:T(8,128)S(1)}, f32[4,6,8,128]{3,2,1,0:T(8,128)}, u32[]{:S(2)}) copy-start(f32[4,6,8,128]{3,2,1,0:T(8,128)} %init_hbm.1) | copy-start | bytes 294916
  2.6 0.7 %copy-start.2 = (f32[6,8,128]{2,1,0:T(8,128)S(1)}, f32[6,8,128]{2,1,0:T(8,128)}, u32[]{:S(2)}) copy-start(f32[6,8,128]{2,1,0:T(8,128)} %shear_hbm.1) | copy-start | bytes 73732
  3.3 0.7 %copy-start.3 = (f32[6,8,128]{2,1,0:T(8,128)S(1)}, f32[6,8,128]{2,1,0:T(8,128)}, u32[]{:S(2)}) copy-start(f32[6,8,128]{2,1,0:T(8,128)} %mobil_hbm.1) | copy-start | bytes 73732

commit v2 on v1

--- a/solution.py
+++ b/solution.py
@@ -157,7 +157,7 @@
     halo,
     face_out,
     face_in,
-    error,
+    image,
     coarse_out,
     coarse_in,
     last_in,
@@ -174,6 +174,8 @@
     face_recv,
     coarse_send,
     coarse_recv,
+    ready,
+    later_ready,
 ):
     integral, widths = node_tables()
     table = [[integral[m][j] - (widths[m] if j == m else 0.0) for j in range(5)] for m in range(4)]
@@ -181,12 +183,24 @@
     t, s = lax.axis_index("tm"), lax.axis_index("space")
     before, after = (lax.rem(t + slices - 1, slices), s), (lax.rem(t + 1, slices), s)
     below, above = (t, lax.rem(s + slabs - 1, slabs)), (t, lax.rem(s + 1, slabs))
-    has_below, has_above, is_first = s > 0, s < slabs - 1, t == 0
+    below_before, below_after = (before[0], below[1]), (after[0], below[1])
+    above_before, above_after = (before[0], above[1]), (after[0], above[1])
+    has_below, has_above, has_before, has_after = s > 0, s < slabs - 1, t > 0, t < slices - 1
     exists = (has_below, has_above)
 
+    place = lax.rem(s, 4)
+    greets = (
+        jnp.logical_or(place == 0, place == 3),
+        jnp.logical_or(place == 0, place == 1),
+    )
+    leads = tuple(jnp.logical_and(exists[side], greets[side]) for side in range(2))
+    follows = tuple(jnp.logical_and(exists[side], jnp.logical_not(greets[side])) for side in range(2))
     barrier = pltpu.get_barrier_semaphore()
-    for device in (before, below, above):
-        pl.semaphore_signal(barrier, inc=1, device_id=device, device_id_type=MESH)
+    for wanted, device in ((has_before, before), (leads[0], below), (leads[1], above)):
+
+        @pl.when(wanted)
+        def _():
+            pl.semaphore_signal(barrier, inc=1, device_id=device, device_id_type=MESH)
 
     loads = [
         pltpu.make_async_copy(old_hbm.at[0], old, local_sem.at[0]),
@@ -212,25 +226,56 @@
         for k in range(FIELD):
             fu[m, k] = images[k]
 
-    pl.semaphore_wait(barrier, 3)
+    greeted = [jnp.where(c, 1, 0) for c in (has_after,) + follows]
+    greeted = greeted[0] + greeted[1] + greeted[2]
+
+    @pl.when(greeted > 0)
+    def _():
+        pl.semaphore_wait(barrier, greeted)
 
     def remote(src, dst, send, recv, device):
         return pltpu.make_async_remote_copy(
             src_ref=src, dst_ref=dst, send_sem=send, recv_sem=recv, device_id=device, device_id_type=MESH
         )
 
+    def start_if(wanted, *copies):
+        @pl.when(wanted)
+        def _():
+            for copy in copies:
+                copy.start()
+
+    def wait_if(wanted, *copies):
+        @pl.when(wanted)
+        def _():
+            for copy in copies:
+                copy.wait_recv()
+
     start_copy = remote(old.at[4], start_in, tm_send.at[0], tm_recv.at[0], after)
-    start_copy.start()
+    start_if(has_after, start_copy)
     coef_copies = [
         remote(coef.at[:, pl.ds(3, 3)], coef_in.at[1], coef_send.at[0], coef_recv.at[1], below),
         remote(coef.at[:, pl.ds(6, 3)], coef_in.at[0], coef_send.at[1], coef_recv.at[0], above),
     ]
-    for copy in coef_copies:
-        copy.start()
-
-    start_copy.wait_recv()
+    for side, device in ((0, below), (1, above)):
+
+        @pl.when(follows[side])
+        def _():
+            pl.semaphore_signal(ready.at[1 - side], inc=1, device_id=device, device_id_type=MESH)
+            coef_copies[side].start()
+
+        @pl.when(jnp.logical_not(exists[side]))
+        def _():
+            face_in[side] = jnp.zeros((5, FIELD, 8, 128), jnp.float32)
+            coef_in[side] = jnp.zeros((2, 3, 8, 128), jnp.float32)
+            coarse_in[:, side] = jnp.zeros((2, 3, 8, 128), jnp.float32)
+
+    @pl.when(jnp.logical_not(has_before))
+    def _():
+        start_in[...] = init[...]
+
+    wait_if(has_before, start_copy)
     for k in range(FIELD):
-        first = jnp.where(is_first, init[k], start_in[k])
+        first = start_in[k]
         node[0, k] = first
         primed[k] = padded(first)
     writes = [pltpu.make_async_copy(node.at[0], new_hbm.at[0, 0], write_sem.at[0])]
@@ -254,7 +299,7 @@
                 face_recv.at[1 - side, m],
                 device,
             )
-            copy.start()
+            start_if(follows[side], copy)
             face_copies.append(copy)
         images = operator([primed[k] for k in range(FIELD)], stiff, fluid, 0.25, 1)
         for k in range(FIELD):
@@ -262,13 +307,22 @@
             primed[k, 1 : 1 + LAYERS] = moved
             if m == 0:
                 node[1, k] = moved
-                error[0, k] = images[k]
-
-    for copy in coef_copies:
-        copy.wait_recv()
-    for array in range(2):
-        coef[array, 0:3] = jnp.where(has_below, coef_in[0, array], 0.0)
-        coef[array, 9:12] = jnp.where(has_above, coef_in[1, array], 0.0)
+                image[k] = images[k]
+
+    for side in (1, 0):
+
+        @pl.when(leads[side])
+        def _():
+            pl.semaphore_wait(ready.at[side], 1)
+            coef_copies[side].start()
+            for m in range(4):
+                face_copies[2 * m + side].start()
+
+    for side in range(2):
+        wait_if(exists[side], coef_copies[1 - side])
+        for array in range(2):
+            lo = (0, 9)[side]
+            coef[array, lo : lo + 3] = coef_in[side, array]
     gradients = [jnp.where(exists[side], 0.25, 0.0) for side in range(2)]
 
     def across(q, side):
@@ -294,20 +348,25 @@
             face_recv.at[1 - side, 4],
             device,
         )
-        copy.start()
+        start_if(exists[side], copy)
         face_copies.append(copy)
 
     def inflow(side, m):
         layer = (3, 8)[side]
-        q = [jnp.where(exists[side], face_in[side, m, k], 0.0)[None] for k in range(FIELD)]
+        q = [face_in[side, m, k][None] for k in range(FIELD)]
         reach = (from_below, from_above)[side]
         return reach(q, coef[0, layer : layer + 1], coef[1, layer : layer + 1], 0.25)
 
     def edge(m, side):
         return [u[m, k, (0, LAYERS - 1)[side]][None] for k in range(FIELD)]
 
-    for side in range(2):
-        face_copies[side].wait_recv()
+    for side, device in ((0, below_before), (1, above_before)):
+        wait_if(exists[side], face_copies[1 - side])
+
+        @pl.when(jnp.logical_and(exists[side], has_before))
+        def _():
+            pl.semaphore_signal(later_ready.at[1 - side], inc=1, device_id=device, device_id_type=MESH)
+
     low, high = inflow(0, 0), inflow(1, 0)
     zero = jnp.zeros((2, 8, 128), jnp.float32)
     out_low = across([face_out[0, 0, k][None] for k in range(FIELD)], 0)
@@ -317,7 +376,7 @@
         halo[0, k] = jnp.concatenate([zero, out_low[k]], axis=0)
         halo[1, k] = jnp.concatenate([out_high[k], zero], axis=0)
 
-    sums = [means([layer_pairs(error[0, k]) for k in range(FIELD)])]
+    sums = [means([layer_pairs(image[k]) for k in range(FIELD)])]
     grad = jnp.concatenate(
         [
             jnp.full((3, 8, 128), 1.0, jnp.float32) * gradients[0],
@@ -344,7 +403,7 @@
         if m == 4:
             break
         for side in range(2):
-            face_copies[2 * m + side].wait_recv()
+            wait_if(exists[side], face_copies[2 * m + 1 - side])
         low, high = inflow(0, m), inflow(1, m)
         out_low, out_high = across(edge(m, 0), 0), across(edge(m, 1), 1)
         for k in range(FIELD):
@@ -355,11 +414,9 @@
             inner = halo[1, k, :reach] + widths[m] * images[k][reach + LAYERS :]
             halo[1, k, :reach] = jnp.concatenate([inner[:1] + out_high[k], inner[1:]], axis=0) if reach > 1 else inner + out_high[k]
 
-    last_copy = remote(node.at[4], last_in, tm_send.at[1], tm_recv.at[1], after)
-    last_copy.start()
-
     for side in range(2):
-        face_copies[8 + side].wait_recv()
+        wait_if(exists[side], face_copies[9 - side])
+    errors = []
     for m in range(4):
         total = table[m][0] * sums[0]
         for j in range(1, 5):
@@ -367,16 +424,21 @@
         total = total - means([layer_pairs(fu[m, k]) for k in range(FIELD)])
         total = ends(
             total,
-            jnp.where(has_below, face_in[0, 4, m], 0.0)[None],
-            jnp.where(has_above, face_in[1, 4, m], 0.0)[None],
+            face_in[0, 4, m][None],
+            face_in[1, 4, m][None],
         )
-        spread_out = spread(total)
-        for k in range(FIELD):
-            error[m, k, 0:3] = spread_out[k]
+        end_out[m] = total
+        errors.append(spread(total))
 
     def coarse_coef(lo, pairs):
         both = [
-            jnp.concatenate([coef[a, lo + 2 * i : lo + 2 * i + 1] + coef[a, lo + 2 * i + 1 : lo + 2 * i + 2] for i in range(pairs)], axis=0)
+            jnp.concatenate(
+                [
+                    coef[a, lo + 2 * i : lo + 2 * i + 1] + coef[a, lo + 2 * i + 1 : lo + 2 * i + 2]
+                    for i in range(pairs)
+                ],
+                axis=0,
+            )
             for a in range(2)
         ]
         pieces = spread(means([both[0], both[0], both[1], both[1]]))
@@ -387,29 +449,48 @@
     coarse_grad = jnp.concatenate([weight[0:1], weight[1:4], weight[7:8]], axis=0)
     own_stiff, own_fluid = coarse_stiff[1:4], coarse_fluid[1:4]
 
-    def send_coarse(m, d):
+    def sweep_alone(e):
+        d = [[e[0][k] for k in range(FIELD)]]
+        for m in (1, 2):
+            images = operator([padded(v) for v in d[-1]], own_stiff, own_fluid, 0.125, 2)
+            d.append([d[-1][k] + widths[m] * images[k] + e[m][k] for k in range(FIELD)])
+        return d
+
+    alone = sweep_alone(errors)
+    for m in range(3):
         for side, layer in ((0, 0), (1, 2)):
-            coarse_out[side, m] = woven([d[k][layer : layer + 1] for k in range(FIELD)])[0]
-
-    d1 = [error[0, k, 0:3] for k in range(FIELD)]
-    send_coarse(0, d1)
-    f1 = operator([padded(v) for v in d1], own_stiff, own_fluid, 0.125, 2)
-    d2 = [d1[k] + widths[1] * f1[k] + error[1, k, 0:3] for k in range(FIELD)]
-    send_coarse(1, d2)
-    f2 = operator([padded(v) for v in d2], own_stiff, own_fluid, 0.125, 2)
-    d3 = [d2[k] + widths[2] * f2[k] + error[2, k, 0:3] for k in range(FIELD)]
-    send_coarse(2, d3)
+            coarse_out[side, m] = woven([alone[m][k][layer : layer + 1] for k in range(FIELD)])[0]
+    end_copies = [remote(end_out, end_in, tm_send.at[2], tm_recv.at[2], after)]
     coarse_copies = []
-    for side, device in ((0, below), (1, above)):
-        copy = remote(
-            coarse_out.at[side],
-            coarse_in.at[1 - side],
-            coarse_send.at[side],
-            coarse_recv.at[1 - side],
-            device,
+    for side, device, later in ((0, below, below_after), (1, above, above_after)):
+        coarse_copies.append(
+            remote(
+                coarse_out.at[side],
+                coarse_in.at[0, 1 - side],
+                coarse_send.at[0, side],
+                coarse_recv.at[0, 1 - side],
+                device,
+            )
         )
-        copy.start()
-        coarse_copies.append(copy)
+        end_copies.append(
+            remote(
+                coarse_out.at[side],
+                coarse_in.at[1, 1 - side],
+                coarse_send.at[1, side],
+                coarse_recv.at[1, 1 - side],
+                later,
+            )
+        )
+    for side in range(2):
+        start_if(exists[side], coarse_copies[side])
+    last_copy = remote(node.at[4], last_in, tm_send.at[1], tm_recv.at[1], after)
+    start_if(has_after, end_copies[0], last_copy)
+    for side in range(2):
+
+        @pl.when(jnp.logical_and(exists[side], has_after))
+        def _():
+            pl.semaphore_wait(later_ready.at[side], 1)
+            end_copies[1 + side].start()
 
     def finish(m, d):
         for k in range(FIELD):
@@ -418,7 +499,7 @@
         write.start()
         writes.append(write)
 
-    finish(1, d1)
+    finish(1, alone[0])
 
     def coarse_across(q, side):
         layer = (0, 4)[side]
@@ -426,51 +507,67 @@
         part = slice(layer, layer + 1)
         return reach(q, coarse_stiff[part], coarse_fluid[part], coarse_grad[part])
 
-    halo_low = [widths[1] * v for v in coarse_across([v[0:1] for v in d1], 0)]
-    halo_high = [widths[1] * v for v in coarse_across([v[2:3] for v in d1], 1)]
-
-    for copy in coarse_copies:
-        copy.wait_recv()
-    coming = [
-        [spread(jnp.where(exists[side], coarse_in[side, m], 0.0)[None]) for m in range(3)] for side in range(2)
-    ]
-
-    def coarse_inflow(m):
-        low = from_below(coming[0][m], own_stiff[0:1], own_fluid[0:1], 0.125)
-        high = from_above(coming[1][m], own_stiff[2:3], own_fluid[2:3], 0.125)
-        return low, high
-
-    low, high = coarse_inflow(0)
-    d2 = [ends(d2[k], widths[1] * low[k], widths[1] * high[k]) for k in range(FIELD)]
+    def sweep(e, d, slot, arrivals):
+        d1, d2 = d[0], d[1]
+        halo_low = [widths[1] * v for v in coarse_across([v[0:1] for v in d1], 0)]
+        halo_high = [widths[1] * v for v in coarse_across([v[2:3] for v in d1], 1)]
+        for side in range(2):
+            wait_if(exists[side], arrivals[1 - side])
+        coming = [
+            [spread(coarse_in[slot, side, m][None]) for m in range(3)]
+            for side in range(2)
+        ]
+
+        def coarse_inflow(m):
+            low = from_below(coming[0][m], own_stiff[0:1], own_fluid[0:1], 0.125)
+            high = from_above(coming[1][m], own_stiff[2:3], own_fluid[2:3], 0.125)
+            return low, high
+
+        low, high = coarse_inflow(0)
+        d2 = [ends(d2[k], widths[1] * low[k], widths[1] * high[k]) for k in range(FIELD)]
+        low, high = coarse_inflow(1)
+        q = [padded(jnp.concatenate([halo_low[k], d2[k], halo_high[k]], axis=0)) for k in range(FIELD)]
+        images = operator(q, coarse_stiff, coarse_fluid, coarse_grad, 2)
+        d3 = [
+            d2[k] + widths[2] * ends(images[k][1:4], low[k], high[k]) + e[2][k] for k in range(FIELD)
+        ]
+        halo_low = [halo_low[k] + widths[2] * images[k][0:1] for k in range(FIELD)]
+        halo_high = [halo_high[k] + widths[2] * images[k][4:5] for k in range(FIELD)]
+        halo_low = [halo_low[k] + coming[0][2][k] for k in range(FIELD)]
+        halo_high = [halo_high[k] + coming[1][2][k] for k in range(FIELD)]
+        q = [jnp.concatenate([halo_low[k], d3[k], halo_high[k]], axis=0) for k in range(FIELD)]
+        images = operator(q, own_stiff, own_fluid, 0.125, 2)
+        d4 = [d3[k] + widths[3] * images[k] + e[3][k] for k in range(FIELD)]
+        return d2, d3, d4
+
+    d2, d3, d4 = sweep(errors, alone, 0, coarse_copies)
     finish(2, d2)
-    low, high = coarse_inflow(1)
-    q = [padded(jnp.concatenate([halo_low[k], d2[k], halo_high[k]], axis=0)) for k in range(FIELD)]
-    images = operator(q, coarse_stiff, coarse_fluid, coarse_grad, 2)
-    d3 = [
-        d2[k] + widths[2] * ends(images[k][1:4], low[k], high[k]) + error[2, k, 0:3] for k in range(FIELD)
-    ]
     finish(3, d3)
-    halo_low = [halo_low[k] + widths[2] * images[k][0:1] + coming[0][2][k] for k in range(FIELD)]
-    halo_high = [halo_high[k] + widths[2] * images[k][4:5] + coming[1][2][k] for k in range(FIELD)]
-    q = [jnp.concatenate([halo_low[k], d3[k], halo_high[k]], axis=0) for k in range(FIELD)]
-    images = operator(q, own_stiff, own_fluid, 0.125, 2)
-    d4 = [d3[k] + widths[3] * images[k] + error[3, k, 0:3] for k in range(FIELD)]
-    end_out[...] = woven(d4)
-    end_copy = remote(end_out, end_in, tm_send.at[2], tm_recv.at[2], after)
-    end_copy.start()
     finish(4, d4)
 
-    last_copy.wait_recv()
-    end_copy.wait_recv()
-    d4 = spread(end_in[...])
-    for k in range(FIELD):
-        start_in[k] = jnp.where(is_first, init[k], last_in[k] + twice(d4[k]))
+    @pl.when(has_before)
+    def _():
+        end_copies[0].wait_recv()
+        errors = [spread(end_in[m]) for m in range(4)]
+        d4 = sweep(errors, sweep_alone(errors), 1, end_copies[1:])[2]
+        last_copy.wait_recv()
+        for k in range(FIELD):
+            start_in[k] = last_in[k] + twice(d4[k])
+
     write = pltpu.make_async_copy(start_in, next_hbm.at[0], write_sem.at[5])
     write.start()
     writes.append(write)
 
-    for copy in [start_copy, last_copy, end_copy] + coef_copies + face_copies + coarse_copies:
-        copy.wait_send()
+    def sent_if(wanted, *copies):
+        @pl.when(wanted)
+        def _():
+            for copy in copies:
+                copy.wait_send()
+
+    sent_if(has_after, start_copy, last_copy, end_copies[0])
+    for side in range(2):
+        sent_if(exists[side], coef_copies[side], coarse_copies[side], *face_copies[side::2])
+        sent_if(jnp.logical_and(exists[side], has_after), end_copies[1 + side])
     for write in writes:
         write.wait()
 
@@ -486,7 +583,7 @@
             jax.ShapeDtypeStruct((1, 5, FIELD, LAYERS, 8, 128), jnp.float32),
             jax.ShapeDtypeStruct((1, FIELD, LAYERS, 8, 128), jnp.float32),
         ),
-        in_specs=[pl.BlockSpec(memory_space=pl.ANY)] * 4,
+        in_specs=[pl.BlockSpec(memory_space=pltpu.HBM)] * 4,
         out_specs=(pl.BlockSpec(memory_space=pl.ANY),) * 2,
         scratch_shapes=[
             vmem(5, FIELD, LAYERS),
@@ -502,12 +599,12 @@
             vmem(2, FIELD, 3),
             vmem(2, 5, FIELD),
             vmem(2, 5, FIELD),
-            vmem(4, FIELD, LAYERS),
+            vmem(FIELD, LAYERS),
             vmem(2, 3),
-            vmem(2, 3),
+            vmem(2, 2, 3),
             vmem(FIELD, LAYERS),
-            vmem(3),
-            vmem(3),
+            vmem(4, 3),
+            vmem(4, 3),
             vmem(4, FIELD, LAYERS),
             dma((4,)),
             dma((6,)),
@@ -517,11 +614,13 @@
             dma((2,)),
             dma((2, 5)),
             dma((2, 5)),
-            dma((2,)),
-            dma((2,)),
+            dma((2, 2)),
+            dma((2, 2)),
+            pltpu.SemaphoreType.REGULAR((2,)),
+            pltpu.SemaphoreType.REGULAR((2,)),
         ],
         compiler_params=pltpu.CompilerParams(
-            collective_id=0, has_side_effects=True, vmem_limit_bytes=32 * 1024 * 1024
+            collective_id=0, has_side_effects=True, vmem_limit_bytes=63 * 1024 * 1024
         ),
     )(old_nodes, initial, shear_modulus, mobility)
 

time: 44.5 us -> 41.1 us (0.924)
  the two profiles are of different devices: /device:TPU:1 before, /device:TPU:30 now
where the time goes in v2:
time: 41.1 us; the launch traced here: 40.9 us
  Pallas kernels  37.7 us (92%)
  local copies, waits for them, and re-layouts  2.52 us (6%)
  between operations  0.65 us (2%)
    pallas_call x1, Pallas kernels, on_device(): pl.pallas_call(functools.partial(kernel, counts), out_shape=(jax.ShapeDty...  37.7 us
    unnamed x4, local copies, waits for them, and re-layouts  2.52 us

profile of v2, /device:TPU:30, one launch (start us, length us, event | category | flops | bytes accessed | tf_op | source)
XLA Modules:
  0.0 40.9 jit_solution(13865187392861449375)
XLA Ops:
  0.6 37.7 %shard_map.59 = (f32[1,5,4,6,8,128]{5,4,3,2,1,0:T(8,128)}, f32[1,4,6,8,128]{4,3,2,1,0:T(8,128)}) custom-call(f32[1,5,4,6,8,128]{5,4,3,2,1,0:T(8,128)} %old_hbm.1, f32[4,6,8,128]{3,2,1,0:T(8,128)} %init_hbm.1, f32[6,8,128]{2,1,0:T(8,128)} %shear_hbm.1, f32[6,8,128]{2,1,0:T(8,128)} %mobil_hbm.1), custom_call_target="tpu_custom_call" | custom-call | tf_op jit(solution)/shard_map/pallas_call | solution.py:580
  38.4 0.0 copy-start
  38.4 1.9 %copy.8 = f32[1,5,4,6,8,128]{5,4,3,2,1,0:T(8,128)} copy(f32[1,5,4,6,8,128]{5,4,3,2,1,0:T(8,128)} %get-tuple-element.4) | data formatting | bytes 983040
  40.3 0.0 copy-done
  40.3 0.6 %copy.9 = f32[1,4,6,8,128]{4,3,2,1,0:T(8,128)} copy(f32[1,4,6,8,128]{4,3,2,1,0:T(8,128)S(1)} %copy-done) | data formatting | bytes 196608
Async XLA Ops:
  38.4 1.9 %copy-start = (f32[1,4,6,8,128]{4,3,2,1,0:T(8,128)S(1)}, f32[1,4,6,8,128]{4,3,2,1,0:T(8,128)}, u32[]{:S(2)}) copy-start(f32[1,4,6,8,128]{4,3,2,1,0:T(8,128)} %get-tuple-element.5) | copy-start | bytes 294916

commit v3 on v2

--- a/solution.py
+++ b/solution.py
@@ -139,9 +139,7 @@
 def kernel(
     counts,
     old_hbm,
-    init_hbm,
-    shear_hbm,
-    mobil_hbm,
+    rest_hbm,
     new_hbm,
     next_hbm,
     old,
@@ -183,8 +181,7 @@
     t, s = lax.axis_index("tm"), lax.axis_index("space")
     before, after = (lax.rem(t + slices - 1, slices), s), (lax.rem(t + 1, slices), s)
     below, above = (t, lax.rem(s + slabs - 1, slabs)), (t, lax.rem(s + 1, slabs))
-    below_before, below_after = (before[0], below[1]), (after[0], below[1])
-    above_before, above_after = (before[0], above[1]), (after[0], above[1])
+    below_after, above_after = (after[0], below[1]), (after[0], above[1])
     has_below, has_above, has_before, has_after = s > 0, s < slabs - 1, t > 0, t < slices - 1
     exists = (has_below, has_above)
 
@@ -204,9 +201,9 @@
 
     loads = [
         pltpu.make_async_copy(old_hbm.at[0], old, local_sem.at[0]),
-        pltpu.make_async_copy(shear_hbm, coef.at[0, pl.ds(3, LAYERS)], local_sem.at[1]),
-        pltpu.make_async_copy(mobil_hbm, coef.at[1, pl.ds(3, LAYERS)], local_sem.at[2]),
-        pltpu.make_async_copy(init_hbm, init, local_sem.at[3]),
+        pltpu.make_async_copy(rest_hbm.at[FIELD], coef.at[0, pl.ds(3, LAYERS)], local_sem.at[1]),
+        pltpu.make_async_copy(rest_hbm.at[FIELD + 1], coef.at[1, pl.ds(3, LAYERS)], local_sem.at[2]),
+        pltpu.make_async_copy(rest_hbm.at[pl.ds(0, FIELD)], init, local_sem.at[3]),
     ]
     for load in loads:
         load.start()
@@ -253,8 +250,12 @@
     start_copy = remote(old.at[4], start_in, tm_send.at[0], tm_recv.at[0], after)
     start_if(has_after, start_copy)
     coef_copies = [
-        remote(coef.at[:, pl.ds(3, 3)], coef_in.at[1], coef_send.at[0], coef_recv.at[1], below),
-        remote(coef.at[:, pl.ds(6, 3)], coef_in.at[0], coef_send.at[1], coef_recv.at[0], above),
+        remote(coef.at[:, pl.ds(3, 1)], coef_in.at[1, :, pl.ds(0, 1)], coef_send.at[0, 0], coef_recv.at[0, 1], below),
+        remote(coef.at[:, pl.ds(8, 1)], coef_in.at[0, :, pl.ds(2, 1)], coef_send.at[0, 1], coef_recv.at[0, 0], above),
+    ]
+    deep_copies = [
+        remote(coef.at[:, pl.ds(4, 1)], coef_in.at[1, :, pl.ds(1, 1)], coef_send.at[1, 0], coef_recv.at[1, 1], below),
+        remote(coef.at[:, pl.ds(7, 1)], coef_in.at[0, :, pl.ds(1, 1)], coef_send.at[1, 1], coef_recv.at[1, 0], above),
     ]
     for side, device in ((0, below), (1, above)):
 
@@ -262,6 +263,7 @@
         def _():
             pl.semaphore_signal(ready.at[1 - side], inc=1, device_id=device, device_id_type=MESH)
             coef_copies[side].start()
+            deep_copies[side].start()
 
         @pl.when(jnp.logical_not(exists[side]))
         def _():
@@ -274,6 +276,18 @@
         start_in[...] = init[...]
 
     wait_if(has_before, start_copy)
+
+    def pass_on(side):
+        @pl.when(has_before)
+        def _():
+            pl.semaphore_signal(later_ready.at[side], inc=1, device_id=before, device_id_type=MESH)
+
+    for side in range(2):
+
+        @pl.when(follows[side])
+        def _():
+            pass_on(side)
+
     for k in range(FIELD):
         first = start_in[k]
         node[0, k] = first
@@ -315,14 +329,18 @@
         def _():
             pl.semaphore_wait(ready.at[side], 1)
             coef_copies[side].start()
-            for m in range(4):
-                face_copies[2 * m + side].start()
+            face_copies[side].start()
+            pass_on(side)
+            face_copies[2 + side].start()
+            deep_copies[side].start()
+            face_copies[4 + side].start()
+            face_copies[6 + side].start()
 
     for side in range(2):
         wait_if(exists[side], coef_copies[1 - side])
         for array in range(2):
-            lo = (0, 9)[side]
-            coef[array, lo : lo + 3] = coef_in[side, array]
+            lo, layer = ((2, 2), (9, 0))[side]
+            coef[array, lo : lo + 1] = coef_in[side, array, layer : layer + 1]
     gradients = [jnp.where(exists[side], 0.25, 0.0) for side in range(2)]
 
     def across(q, side):
@@ -360,13 +378,8 @@
     def edge(m, side):
         return [u[m, k, (0, LAYERS - 1)[side]][None] for k in range(FIELD)]
 
-    for side, device in ((0, below_before), (1, above_before)):
+    for side in range(2):
         wait_if(exists[side], face_copies[1 - side])
-
-        @pl.when(jnp.logical_and(exists[side], has_before))
-        def _():
-            pl.semaphore_signal(later_ready.at[1 - side], inc=1, device_id=device, device_id_type=MESH)
-
     low, high = inflow(0, 0), inflow(1, 0)
     zero = jnp.zeros((2, 8, 128), jnp.float32)
     out_low = across([face_out[0, 0, k][None] for k in range(FIELD)], 0)
@@ -386,18 +399,20 @@
         axis=0,
     )
     for m in range(1, 5):
-        reach = (0, 2, 3, 1, 0)[m]
+        if m == 1:
+            for side in range(2):
+                wait_if(exists[side], deep_copies[1 - side])
+                for array in range(2):
+                    lo = (1, 10)[side]
+                    coef[array, lo : lo + 1] = coef_in[side, array, 1:2]
+        reach = (0, 2, 2, 1, 0)[m]
         own = slice(reach, reach + LAYERS)
         lo, hi = 3 - reach, 9 + reach
         q = []
         for k in range(FIELD):
-            if reach == 3:
-                whole = padded(jnp.concatenate([halo[0, k], node[m, k], halo[1, k]], axis=0))
-            else:
-                whole = jnp.concatenate(
-                    [halo[0, k, 2 - reach :], node[m, k], halo[1, k, : reach + 1]], axis=0
-                )
-            q.append(whole)
+            q.append(
+                jnp.concatenate([halo[0, k, 2 - reach :], node[m, k], halo[1, k, : reach + 1]], axis=0)
+            )
         images = operator(q, coef[0, lo:hi], coef[1, lo:hi], grad[lo:hi], 1)
         sums.append(means([layer_pairs(images[k][own]) for k in range(FIELD)]))
         if m == 4:
@@ -566,7 +581,7 @@
 
     sent_if(has_after, start_copy, last_copy, end_copies[0])
     for side in range(2):
-        sent_if(exists[side], coef_copies[side], coarse_copies[side], *face_copies[side::2])
+        sent_if(exists[side], coef_copies[side], deep_copies[side], coarse_copies[side], *face_copies[side::2])
         sent_if(jnp.logical_and(exists[side], has_after), end_copies[1 + side])
     for write in writes:
         write.wait()
@@ -583,7 +598,7 @@
             jax.ShapeDtypeStruct((1, 5, FIELD, LAYERS, 8, 128), jnp.float32),
             jax.ShapeDtypeStruct((1, FIELD, LAYERS, 8, 128), jnp.float32),
         ),
-        in_specs=[pl.BlockSpec(memory_space=pltpu.HBM)] * 4,
+        in_specs=[pl.BlockSpec(memory_space=pltpu.HBM)] * 2,
         out_specs=(pl.BlockSpec(memory_space=pl.ANY),) * 2,
         scratch_shapes=[
             vmem(5, FIELD, LAYERS),
@@ -610,8 +625,8 @@
             dma((6,)),
             dma((3,)),
             dma((3,)),
-            dma((2,)),
-            dma((2,)),
+            dma((2, 2)),
+            dma((2, 2)),
             dma((2, 5)),
             dma((2, 5)),
             dma((2, 2)),
@@ -620,9 +635,9 @@
             pltpu.SemaphoreType.REGULAR((2,)),
         ],
         compiler_params=pltpu.CompilerParams(
-            collective_id=0, has_side_effects=True, vmem_limit_bytes=63 * 1024 * 1024
+            collective_id=0, has_side_effects=True, vmem_limit_bytes=54400 * 1024
         ),
-    )(old_nodes, initial, shear_modulus, mobility)
+    )(old_nodes, jnp.concatenate([initial, shear_modulus[None], mobility[None]], axis=0))
 
 
 def solution(mesh):

time: 41.1 us -> 39.8 us (0.968)
  the two profiles are of different devices: /device:TPU:30 before, /device:TPU:8 now
where the time goes in v3:
time: 39.8 us; the launch traced here: 39.6 us
  Pallas kernels  36.6 us (92%)
  local copies, waits for them, and re-layouts  1.42 us (4%)
  other arithmetic  0.94 us (2%)
  between operations  0.64 us (2%)
    pallas_call x1, Pallas kernels, on_device(): pl.pallas_call(functools.partial(kernel, counts), out_shape=(jax.ShapeDty...  36.6 us
    unnamed x2, local copies, waits for them, and re-layouts  1.42 us
    concatenate x1, other arithmetic, on_device(): jnp.concatenate([initial, shear_modulus[None], mobility[None]], axis=0)  0.94 us

profile of v3, /device:TPU:8, one launch (start us, length us, event | category | flops | bytes accessed | tf_op | source)
XLA Modules:
  0.0 39.6 jit_solution(5456797723579092620)
XLA Ops:
  0.6 0.9 %pad_maximum_fusion.rest_hbm = f32[6,6,8,128]{3,2,1,0:T(8,128)S(1)} fusion(f32[1,6,8,128]{3,2,1,0:T(8,128)} %bitcast.2, f32[1,6,8,128]{3,2,1,0:T(8,128)} %bitcast.3, f32[4,6,8,128]{3,2,1,0:T(8,128)} %param.5), kind=kLoop, calls=%fused_computation | loop fusion | flops 73728 | bytes 294912 | tf_op jit(solution)/shard_map/concatenate | solution.py:640
  1.6 36.6 %shard_map.59 = (f32[1,5,4,6,8,128]{5,4,3,2,1,0:T(8,128)S(1)}, f32[1,4,6,8,128]{4,3,2,1,0:T(8,128)S(1)}) custom-call(f32[1,5,4,6,8,128]{5,4,3,2,1,0:T(8,128)} %old_hbm.1, f32[6,6,8,128]{3,2,1,0:T(8,128)S(1)} %pad_maximum_fusion.rest_hbm), custom_call_target="tpu_custom_call" | custom-call | tf_op jit(solution)/shard_map/pallas_call | solution.py:595
  38.2 0.8 %copy.8 = f32[1,5,4,6,8,128]{5,4,3,2,1,0:T(8,128)} copy(f32[1,5,4,6,8,128]{5,4,3,2,1,0:T(8,128)S(1)} %get-tuple-element.4) | data formatting | bytes 983040
  38.9 0.6 %copy.9 = f32[1,4,6,8,128]{4,3,2,1,0:T(8,128)} copy(f32[1,4,6,8,128]{4,3,2,1,0:T(8,128)S(1)} %get-tuple-element.5) | data formatting | bytes 196608

commit v4 on v3

--- a/solution.py
+++ b/solution.py
@@ -222,6 +222,7 @@
         images = operator([padded(u[m, k]) for k in range(FIELD)], stiff, fluid, 0.25, 1)
         for k in range(FIELD):
             fu[m, k] = images[k]
+        end_out[m] = means([layer_pairs(images[k]) for k in range(FIELD)])
 
     greeted = [jnp.where(c, 1, 0) for c in (has_after,) + follows]
     greeted = greeted[0] + greeted[1] + greeted[2]
@@ -429,21 +430,12 @@
             inner = halo[1, k, :reach] + widths[m] * images[k][reach + LAYERS :]
             halo[1, k, :reach] = jnp.concatenate([inner[:1] + out_high[k], inner[1:]], axis=0) if reach > 1 else inner + out_high[k]
 
-    for side in range(2):
-        wait_if(exists[side], face_copies[9 - side])
-    errors = []
+    partial = []
     for m in range(4):
         total = table[m][0] * sums[0]
         for j in range(1, 5):
             total = total + table[m][j] * sums[j]
-        total = total - means([layer_pairs(fu[m, k]) for k in range(FIELD)])
-        total = ends(
-            total,
-            face_in[0, 4, m][None],
-            face_in[1, 4, m][None],
-        )
-        end_out[m] = total
-        errors.append(spread(total))
+        partial.append(total - end_out[m])
 
     def coarse_coef(lo, pairs):
         both = [
@@ -463,6 +455,14 @@
     weight = 0.5 * grad[2:10]
     coarse_grad = jnp.concatenate([weight[0:1], weight[1:4], weight[7:8]], axis=0)
     own_stiff, own_fluid = coarse_stiff[1:4], coarse_fluid[1:4]
+
+    errors = []
+    for side in range(2):
+        wait_if(exists[side], face_copies[9 - side])
+    for m in range(4):
+        total = ends(partial[m], face_in[0, 4, m][None], face_in[1, 4, m][None])
+        end_out[m] = total
+        errors.append(spread(total))
 
     def sweep_alone(e):
         d = [[e[0][k] for k in range(FIELD)]]

time: 39.8 us -> 39.7 us (level)
  no operation moved by 1% of the time
where the time goes in v4:
time: 39.7 us; the launch traced here: 39.5 us
  Pallas kernels  36.5 us (92%)
  local copies, waits for them, and re-layouts  1.42 us (4%)
  other arithmetic  0.94 us (2%)
  between operations  0.64 us (2%)
    pallas_call x1, Pallas kernels, on_device(): pl.pallas_call(functools.partial(kernel, counts), out_shape=(jax.ShapeDty...  36.5 us
    unnamed x2, local copies, waits for them, and re-layouts  1.42 us
    concatenate x1, other arithmetic, on_device(): jnp.concatenate([initial, shear_modulus[None], mobility[None]], axis=0)  0.94 us

profile of v4, /device:TPU:8, one launch (start us, length us, event | category | flops | bytes accessed | tf_op | source)
XLA Modules:
  0.0 39.5 jit_solution(6361190360318107941)
XLA Ops:
  0.6 0.9 %pad_maximum_fusion.rest_hbm = f32[6,6,8,128]{3,2,1,0:T(8,128)S(1)} fusion(f32[1,6,8,128]{3,2,1,0:T(8,128)} %bitcast.2, f32[1,6,8,128]{3,2,1,0:T(8,128)} %bitcast.3, f32[4,6,8,128]{3,2,1,0:T(8,128)} %param.5), kind=kLoop, calls=%fused_computation | loop fusion | flops 73728 | bytes 294912 | tf_op jit(solution)/shard_map/concatenate | solution.py:640
  1.6 36.5 %shard_map.59 = (f32[1,5,4,6,8,128]{5,4,3,2,1,0:T(8,128)S(1)}, f32[1,4,6,8,128]{4,3,2,1,0:T(8,128)S(1)}) custom-call(f32[1,5,4,6,8,128]{5,4,3,2,1,0:T(8,128)} %old_hbm.1, f32[6,6,8,128]{3,2,1,0:T(8,128)S(1)} %pad_maximum_fusion.rest_hbm), custom_call_target="tpu_custom_call" | custom-call | tf_op jit(solution)/shard_map/pallas_call | solution.py:595
  38.1 0.8 %copy.8 = f32[1,5,4,6,8,128]{5,4,3,2,1,0:T(8,128)} copy(f32[1,5,4,6,8,128]{5,4,3,2,1,0:T(8,128)S(1)} %get-tuple-element.4) | data formatting | bytes 983040
  38.9 0.6 %copy.9 = f32[1,4,6,8,128]{4,3,2,1,0:T(8,128)} copy(f32[1,4,6,8,128]{4,3,2,1,0:T(8,128)S(1)} %get-tuple-element.5) | data formatting | bytes 196608

commit v5 on v4

--- a/solution.py
+++ b/solution.py
@@ -498,8 +498,7 @@
         )
     for side in range(2):
         start_if(exists[side], coarse_copies[side])
-    last_copy = remote(node.at[4], last_in, tm_send.at[1], tm_recv.at[1], after)
-    start_if(has_after, end_copies[0], last_copy)
+    start_if(has_after, end_copies[0])
     for side in range(2):
 
         @pl.when(jnp.logical_and(exists[side], has_after))
@@ -555,6 +554,8 @@
         d4 = [d3[k] + widths[3] * images[k] + e[3][k] for k in range(FIELD)]
         return d2, d3, d4
 
+    last_copy = remote(node.at[4], last_in, tm_send.at[1], tm_recv.at[1], after)
+    start_if(has_after, last_copy)
     d2, d3, d4 = sweep(errors, alone, 0, coarse_copies)
     finish(2, d2)
     finish(3, d3)

time: 39.7 us -> 39.7 us (level)
  no operation moved by 1% of the time
where the time goes in v5:
time: 39.7 us; the launch traced here: 39.5 us
  Pallas kernels  36.5 us (92%)
  local copies, waits for them, and re-layouts  1.42 us (4%)
  other arithmetic  0.94 us (2%)
  between operations  0.64 us (2%)
    pallas_call x1, Pallas kernels, on_device(): pl.pallas_call(functools.partial(kernel, counts), out_shape=(jax.ShapeDty...  36.5 us
    unnamed x2, local copies, waits for them, and re-layouts  1.42 us
    concatenate x1, other arithmetic, on_device(): jnp.concatenate([initial, shear_modulus[None], mobility[None]], axis=0)  0.94 us

profile of v5, /device:TPU:8, one launch (start us, length us, event | category | flops | bytes accessed | tf_op | source)
XLA Modules:
  0.0 39.5 jit_solution(3129218311551910228)
XLA Ops:
  0.6 0.9 %pad_maximum_fusion.rest_hbm = f32[6,6,8,128]{3,2,1,0:T(8,128)S(1)} fusion(f32[1,6,8,128]{3,2,1,0:T(8,128)} %bitcast.2, f32[1,6,8,128]{3,2,1,0:T(8,128)} %bitcast.3, f32[4,6,8,128]{3,2,1,0:T(8,128)} %param.5), kind=kLoop, calls=%fused_computation | loop fusion | flops 73728 | bytes 294912 | tf_op jit(solution)/shard_map/concatenate | solution.py:641
  1.6 36.5 %shard_map.59 = (f32[1,5,4,6,8,128]{5,4,3,2,1,0:T(8,128)S(1)}, f32[1,4,6,8,128]{4,3,2,1,0:T(8,128)S(1)}) custom-call(f32[1,5,4,6,8,128]{5,4,3,2,1,0:T(8,128)} %old_hbm.1, f32[6,6,8,128]{3,2,1,0:T(8,128)S(1)} %pad_maximum_fusion.rest_hbm), custom_call_target="tpu_custom_call" | custom-call | tf_op jit(solution)/shard_map/pallas_call | solution.py:596
  38.1 0.8 %copy.8 = f32[1,5,4,6,8,128]{5,4,3,2,1,0:T(8,128)} copy(f32[1,5,4,6,8,128]{5,4,3,2,1,0:T(8,128)S(1)} %get-tuple-element.4) | data formatting | bytes 983040
  38.9 0.6 %copy.9 = f32[1,4,6,8,128]{4,3,2,1,0:T(8,128)} copy(f32[1,4,6,8,128]{4,3,2,1,0:T(8,128)S(1)} %get-tuple-element.5) | data formatting | bytes 196608
